TPU v7x, 512 devices: a whole 4x8x8 slice. The times are simulated.
512 devices in a mesh: video: 4 (over z_lo), frame: 32 (over x, y), chan: 4 (over z_hi, core).
Axes of the slice: x: 4, y: 8, z: 8 (z_hi: 2, z_lo: 4; z = z_hi * 4 + z_lo), core: 2. Of those that a mesh axis runs over, the one named last changes fastest.
Arguments:
- latents: bfloat16 [128, 320, 3072], P(('video', 'frame'), 'chan'), parts along dimension 0, may hold values from -96 to 96
- time_weight1: bfloat16 [3, 320, 320], replicated, may hold values from -0.1875 to 0.1875
- norm_gain1: float32 [320], P('chan'), may hold values from 0.1 to 1.9
- norm_shift1: float32 [320], P('chan'), may hold values from -3 to 3
- down_weight: bfloat16 [9, 320, 320], P(None, 'chan'), may hold values from -0.109375 to 0.109375
- norm_gain2: float32 [320], replicated, may hold values from 0.1 to 1.9
- norm_shift2: float32 [320], replicated, may hold values from -3 to 3
- conv_weight2: bfloat16 [9, 320, 640], P(None, None, 'chan'), may hold values from -0.109375 to 0.109375
- skip_weight2: bfloat16 [320, 640], P(None, 'chan'), may hold values from -0.3125 to 0.3125
- time_bias2: float32 [640], P('chan'), may hold values from -4 to 4
- time_weight2: bfloat16 [3, 640, 640], replicated, may hold values from -0.125 to 0.125
- norm_gain3: float32 [640], P('chan'), may hold values from 0.1 to 1.9
- norm_shift3: float32 [640], P('chan'), may hold values from -3 to 3
Outputs:
- block_out: bfloat16 [128, 640, 768], P(('video', 'frame'), 'chan'), parts along dimension 0
There are 4 independent parts, one for each index of `video`. A program takes and returns all parts, laid end to end along the dimension named above; an argument that names none is the same for every part. Nothing has to cross between parts.
All inputs are finite; a program needn't handle non-finite values.
Results may differ from a plain program's by a relative error of at most 0.013.
Values may be sent and summed in bfloat16 or wider, within the bound.
A program may use at most 128 MiB of HBM per device.

v0:
```python
import jax
import jax.numpy as jnp
from jax import lax
from jax.sharding import PartitionSpec as P

C1 = 320
GROUPS = 32
W1 = 128
H1 = 24
H2 = 12
W2 = 64


epsilon = 1e-06


def contract(left_side, right_side):
    return lax.dot_general(
        left_side, right_side, (((0,), (0,)), ((), ())), preferred_element_type=jnp.float32
    )


def norm_apply(values, mean_val, mean_sq, gain_vec, shift_vec, group_size):
    channels, positions = values.shape
    grouped = values.reshape(channels // group_size, group_size, positions)
    inverse = lax.rsqrt(mean_sq - mean_val * mean_val + epsilon)
    scaled = (grouped - mean_val[:, None, None]) * inverse[:, None, None]
    scaled = scaled.reshape(channels, positions) * gain_vec[:, None] + shift_vec[:, None]
    return jax.nn.silu(scaled).astype(jnp.bfloat16)


def norm_space(values, gain_vec, shift_vec):
    channels, positions = values.shape
    group_size = C1 // GROUPS
    grouped = values.reshape(channels // group_size, group_size, positions)
    mean_val = jnp.mean(grouped, axis=(1, 2))
    mean_sq = jnp.mean(grouped * grouped, axis=(1, 2))
    return norm_apply(values, mean_val, mean_sq, gain_vec, shift_vec, group_size)


def tap_sum(portion, kernel):
    frames = portion.shape[0]
    padded = jnp.pad(portion, ((1, 1), (0, 0), (0, 0)))
    summed = jnp.einsum(
        "fnq,no->foq", padded[0:frames], kernel[0], preferred_element_type=jnp.float32
    )
    for tap_index in range(1, 3):
        summed = summed + jnp.einsum(
            "fnq,no->foq",
            padded[tap_index : tap_index + frames],
            kernel[tap_index],
            preferred_element_type=jnp.float32,
        )
    return summed


def columns(values, height, breadth, stride):
    channels = values.shape[0]
    grid_view = values.reshape(channels, height, breadth)
    padded = jnp.pad(grid_view, ((0, 0), (1, 1), (1, 1)))
    out_rows = height // stride
    out_cols = breadth // stride
    tap_list = [
        padded[
            :,
            row_off : row_off + stride * out_rows : stride,
            col_off : col_off + stride * out_cols : stride,
        ]
        for row_off in range(3)
        for col_off in range(3)
    ]
    return jnp.stack(tap_list, 0).reshape(9 * channels, out_rows * out_cols)


def time_block(values, weight, gain_vec, shift_vec):
    channels = values.shape[1]
    positions = values.shape[2]
    chan_count = lax.axis_size("chan")
    group_size = channels * chan_count // GROUPS
    widened = values[0].astype(jnp.float32)
    grouped = widened.reshape(channels // group_size, group_size, positions)
    partial_sums = (jnp.sum(grouped, axis=(1, 2)), jnp.sum(grouped * grouped, axis=(1, 2)))
    sum_all, sum_sq = lax.psum((partial_sums[0], partial_sums[1]), "frame")
    counted = group_size * positions * lax.axis_size("frame")
    hidden = norm_apply(
        widened, sum_all / counted, sum_sq / counted, gain_vec, shift_vec, group_size
    )[None]
    relaid = lax.all_to_all(hidden, "frame", split_axis=2, concat_axis=0, tiled=True)
    own_weight = lax.dynamic_slice_in_dim(weight, lax.axis_index("chan") * channels, channels, 2)
    mixed_out = tap_sum(lax.all_gather(relaid, "chan", axis=1, tiled=True), own_weight).astype(
        jnp.bfloat16
    )
    returned = lax.all_to_all(mixed_out, "frame", split_axis=0, concat_axis=2, tiled=True)
    return (values.astype(jnp.float32) + returned.astype(jnp.float32)).astype(jnp.bfloat16)


def per_device(
    latents,
    time_weight1,
    norm_gain1,
    norm_shift1,
    down_weight,
    norm_gain2,
    norm_shift2,
    conv_weight2,
    skip_weight2,
    time_bias2,
    time_weight2,
    norm_gain3,
    norm_shift3,
):
    block_one = time_block(latents, time_weight1, norm_gain1, norm_shift1)
    in_chans = block_one.shape[1]
    stacked = columns(block_one[0], H1, W1, 2)
    flat_weight = down_weight.reshape(9 * in_chans, down_weight.shape[2])
    out_chans = conv_weight2.shape[2]
    reduced = lax.psum_scatter(
        contract(flat_weight, stacked), "chan", scatter_dimension=0, tiled=True
    ).astype(jnp.bfloat16)
    offset_own = lax.axis_index("chan") * in_chans
    gain_own = lax.dynamic_slice_in_dim(norm_gain2, offset_own, in_chans)
    shift_own = lax.dynamic_slice_in_dim(norm_shift2, offset_own, in_chans)
    normed = norm_space(reduced.astype(jnp.float32), gain_own, shift_own)
    reduced_part = lax.all_gather(reduced, "chan", axis=0, tiled=True)
    normed_part = lax.all_gather(normed, "chan", axis=0, tiled=True)
    amount = reduced_part.shape[0]
    kernel = conv_weight2.reshape(9 * amount, out_chans)
    spatial = contract(kernel, columns(normed_part, H2, W2, 1)) + contract(
        skip_weight2, reduced_part
    )
    second = (spatial + time_bias2[:, None]).astype(jnp.bfloat16)[None]
    return time_block(second, time_weight2, norm_gain3, norm_shift3)


def solution(mesh):
    return jax.shard_map(
        per_device,
        mesh=mesh,
        in_specs=(
            P(("video", "frame"), "chan", None),
            P(),
            P("chan"),
            P("chan"),
            P(None, "chan", None),
            P(),
            P(),
            P(None, None, "chan"),
            P(None, "chan"),
            P("chan"),
            P(),
            P("chan"),
            P("chan"),
        ),
        out_specs=P(("video", "frame"), "chan", None),
        check_vma=False,
    )
```

profile of v0, /device:TPU:8, one launch (start us, length us, event | category | flops | bytes accessed | tf_op | source)
XLA Modules:
  0.0 646.7 jit_solution(3304888771317740929)
XLA Ops:
  6.5 1.4 convert_reduce_fusion
  8.4 75.4 %all-reduce.5 = (f32[8]{0:T(128)S(1)}, f32[8]{0:T(128)S(1)}) all-reduce(f32[8]{0:T(128)S(1)} %reduce_sum.77, f32[8]{0:T(128)S(1)} %reduce_sum.74), channel_id=1, replica_groups=mesh['video'=4,'frame'=32,'chan'=4] {'frame'}, use_global_device_ids=true, to_apply=%region_5.6 | all-reduce | flops 16 | bytes 128 | tf_op jit(solution)/shard_map/psum | solution.py:83
  84.1 1.5 fusion.23
  85.7 2.9 copy.63
  89.1 18.0 %reduce.13 = bf16[3072,80]{1,0:T(8,128)(2,1)S(1)} reduce(bf16[3072,1,80]{2,1,0:T(2,128)(2,1)} %bitcast.166, bf16[]{:T(256)} %broadcast.102), dimensions={1}, to_apply=%bitcast.145.reduce_sub_computation | reduce | bytes 983042
  107.1 2.0 reshape.128
  109.1 17.1 %all_to_all.54 = bf16[32,2,3840]{2,1,0:T(2,128)(2,1)S(1)} all-to-all(bf16[32,2,3840]{2,1,0:T(2,128)(2,1)} %reshape.128), channel_id=1, replica_groups=mesh['video'=4,'frame'=32,'chan'=4] {'frame'}, dimensions={0} | all-to-all | bytes 983040 | tf_op jit(solution)/shard_map/all_to_all | solution.py:88
  126.2 2.7 reshape.129
  128.9 3.5 copy.64
  132.4 1.5 all_to_all.41
  134.4 51.0 %all-gather.4.cloned.1.call-done = bf16[32,1,320,96]{3,0,1,2:T(8,128)(2,1)} async-done(((bf16[32,1,80,96]{3,0,1,2:T(8,128)(2,1)}), bf16[32,1,320,96]{3,0,1,2:T(8,128)(2,1)}) %all-gather.4.cloned.1.call-update) | async-done | bytes 1966096 | tf_op jit(solution)/shard_map/all_gather | solution.py:90
  185.4 4.6 copy.66
  190.0 3.2 fusion.2
  193.3 2.2 fusion
  195.5 2.3 fusion.8
  197.8 30.4 %all_to_all.55 = bf16[32,80,96]{2,1,0:T(8,128)(2,1)S(1)} all-to-all(bf16[32,80,96]{2,1,0:T(8,128)(2,1)S(1)} %fusion.8), channel_id=1, replica_groups=mesh['video'=4,'frame'=32,'chan'=4] {'frame'}, dimensions={0} | all-to-all | bytes 983040 | tf_op jit(solution)/shard_map/all_to_all | solution.py:93
  228.3 1.5 copy.67
  229.8 3.1 reshape.116
  232.8 1.3 fusion.42
  234.3 1.8 pad.17
  236.0 10.6 %slice.89 = bf16[80,12,64]{2,1,0:T(8,128)(2,1)} slice(bf16[80,26,130]{2,1,0:T(8,128)(2,1)} %pad.17), slice={[0:80:1], [0:24:2], [0:128:2]} | slice | bytes 245760 | tf_op jit(solution)/shard_map/slice | solution.py:64
  246.6 10.7 %slice.90 = bf16[80,12,64]{2,1,0:T(8,128)(2,1)} slice(bf16[80,26,130]{2,1,0:T(8,128)(2,1)} %pad.17), slice={[0:80:1], [0:24:2], [1:129:2]} | slice | bytes 245760 | tf_op jit(solution)/shard_map/slice | solution.py:64
  257.3 10.7 %slice.91 = bf16[80,12,64]{2,1,0:T(8,128)(2,1)} slice(bf16[80,26,130]{2,1,0:T(8,128)(2,1)} %pad.17), slice={[0:80:1], [0:24:2], [2:130:2]} | slice | bytes 245760 | tf_op jit(solution)/shard_map/slice | solution.py:64
  268.1 10.6 %slice.92 = bf16[80,12,64]{2,1,0:T(8,128)(2,1)} slice(bf16[80,26,130]{2,1,0:T(8,128)(2,1)} %pad.17), slice={[0:80:1], [1:25:2], [0:128:2]} | slice | bytes 245760 | tf_op jit(solution)/shard_map/slice | solution.py:64
  278.7 10.7 %slice.93 = bf16[80,12,64]{2,1,0:T(8,128)(2,1)} slice(bf16[80,26,130]{2,1,0:T(8,128)(2,1)} %pad.17), slice={[0:80:1], [1:25:2], [1:129:2]} | slice | bytes 245760 | tf_op jit(solution)/shard_map/slice | solution.py:64
  289.4 10.7 %slice.94 = bf16[80,12,64]{2,1,0:T(8,128)(2,1)} slice(bf16[80,26,130]{2,1,0:T(8,128)(2,1)} %pad.17), slice={[0:80:1], [1:25:2], [2:130:2]} | slice | bytes 245760 | tf_op jit(solution)/shard_map/slice | solution.py:64
  300.1 10.2 %slice.95 = bf16[80,12,64]{2,1,0:T(8,128)(2,1)S(1)} slice(bf16[80,26,130]{2,1,0:T(8,128)(2,1)} %pad.17), slice={[0:80:1], [2:26:2], [0:128:2]} | slice | bytes 245760 | tf_op jit(solution)/shard_map/slice | solution.py:64
  310.3 10.5 %slice.96 = bf16[80,12,64]{2,1,0:T(8,128)(2,1)S(1)} slice(bf16[80,26,130]{2,1,0:T(8,128)(2,1)} %pad.17), slice={[0:80:1], [2:26:2], [1:129:2]} | slice | bytes 245760 | tf_op jit(solution)/shard_map/slice | solution.py:64
  320.9 10.4 %slice.97 = bf16[80,12,64]{2,1,0:T(8,128)(2,1)S(1)} slice(bf16[80,26,130]{2,1,0:T(8,128)(2,1)} %pad.17), slice={[0:80:1], [2:26:2], [2:130:2]} | slice | bytes 245760 | tf_op jit(solution)/shard_map/slice | solution.py:64
  331.3 1.7 bitcast_dynamic-update-slice_fusion.8
  333.0 1.7 bitcast_dynamic-update-slice_fusion.7
  334.7 1.7 bitcast_dynamic-update-slice_fusion.6
  336.5 1.7 bitcast_dynamic-update-slice_fusion.5
  338.2 1.7 bitcast_dynamic-update-slice_fusion.4
  342.9 4.6 reshape.111
  347.5 2.9 convolution_bitcast_fusion
  352.0 2.6 copy.71
  354.6 38.0 %reduce-scatter.2.cloned.1.call-done = f32[80,768]{1,0:T(8,128)} async-done(((f32[320,768]{1,0:T(8,128)}), f32[80,768]{1,0:T(8,128)}) %reduce-scatter.2.cloned.1.call-update) | async-done | bytes 245776 | tf_op jit(solution)/shard_map/reduce_scatter | solution.py:117
  392.5 1.1 convert_reduce_fusion.1
  394.3 12.7 %all_gather.14 = bf16[320,768]{1,0:T(8,128)(2,1)S(1)} all-gather(bf16[80,768]{1,0:T(8,128)(2,1)S(1)} %get-tuple-element.13), channel_id=1, replica_groups=mesh['video'=4,'frame'=32,'chan'=4] {'chan'}, dimensions={0}, use_global_device_ids=true | all-gather | bytes 614400 | tf_op jit(solution)/shard_map/all_gather | solution.py:124
  407.2 14.1 %all_gather.13 = bf16[320,768]{1,0:T(8,128)(2,1)} all-gather(bf16[80,768]{1,0:T(8,128)(2,1)S(1)} %fusion.56), channel_id=1, replica_groups=mesh['video'=4,'frame'=32,'chan'=4] {'chan'}, dimensions={0}, use_global_device_ids=true | all-gather | bytes 614400 | tf_op jit(solution)/shard_map/all_gather | solution.py:125
  421.3 1.3 copy.68
  422.6 1.0 fusion.27
  424.5 1.0 fusion.31
  425.4 1.0 fusion.33
  427.3 1.0 fusion.35
  428.3 1.0 fusion.37
  431.1 10.4 %copy.70 = bf16[9,320,12,64]{1,0,3,2:T(8,128)(2,1)} copy(bf16[9,320,12,64]{1,3,2,0:T(8,128)(2,1)} %fusion.41) | data formatting | bytes 8847360 | tf_op jit(solution)/shard_map/stack | solution.py:72
  441.5 11.9 %reshape.114 = bf16[2880,768]{0,1:T(8,128)(2,1)} reshape(bf16[9,320,12,64]{1,0,3,2:T(8,128)(2,1)} %copy.70) | data formatting | bytes 8847360 | tf_op jit(solution)/shard_map/reshape | solution.py:72
  453.4 4.4 fusion.72
  458.8 71.2 %all-reduce.4 = (f32[8]{0:T(128)S(1)}, f32[8]{0:T(128)S(1)}) all-reduce(f32[8]{0:T(128)S(1)} %reduce_sum.113, f32[8]{0:T(128)S(1)} %reduce_sum.110), channel_id=1, replica_groups=mesh['video'=4,'frame'=32,'chan'=4] {'frame'}, use_global_device_ids=true, to_apply=%region_16.17 | all-reduce | flops 16 | bytes 128 | tf_op jit(solution)/shard_map/psum | solution.py:83
  530.7 1.8 copy.73
  532.4 4.0 reduce.14
  536.5 1.4 reshape.130
  537.8 7.5 %all-to-all-start.2 = ((bf16[32,2,1920]{2,1,0:T(2,128)(2,1)}), bf16[32,2,1920]{2,1,0:T(2,128)(2,1)S(1)}, u32[]{:S(2)}, u32[]{:S(2)}) async-start(bf16[32,2,1920]{2,1,0:T(2,128)(2,1)} %reshape.130), calls=%async_computation.3 | async-start | bytes 491520 | tf_op jit(solution)/shard_map/all_to_all | solution.py:88
  545.3 10.9 %all-to-all-done.2 = bf16[32,2,1920]{2,1,0:T(2,128)(2,1)S(1)} async-done(((bf16[32,2,1920]{2,1,0:T(2,128)(2,1)}), bf16[32,2,1920]{2,1,0:T(2,128)(2,1)S(1)}, u32[]{:S(2)}, u32[]{:S(2)}) %all-to-all-start.2) | async-done | bytes 245792 | tf_op jit(solution)/shard_map/all_to_all | solution.py:88
  556.2 1.3 reshape.131
  557.6 1.2 copy.78
  558.8 1.5 copy.74
  560.3 47.8 %all-gather.1 = bf16[32,1,640,24]{0,3,1,2:T(8,128)(2,1)} all-gather(bf16[32,1,160,24]{0,3,1,2:T(8,128)(2,1)} %copy.74), channel_id=3, replica_groups=mesh['video'=4,'frame'=32,'chan'=4] {'chan'}, dimensions={2}, use_global_device_ids=true | all-gather | bytes 1228800 | tf_op jit(solution)/shard_map/all_gather | solution.py:90
  608.1 5.4 copy.75
  613.5 1.9 fusion.14
  616.9 19.7 %all_to_all.56 = bf16[32,160,24]{1,2,0:T(8,128)(2,1)S(1)} all-to-all(bf16[32,160,24]{1,2,0:T(8,128)(2,1)S(1)} %copy.76), channel_id=1, replica_groups=mesh['video'=4,'frame'=32,'chan'=4] {'frame'}, dimensions={0} | all-to-all | bytes 491520 | tf_op jit(solution)/shard_map/all_to_all | solution.py:93
  637.5 1.4 copy.77
  (71 shorter events, 15.5 us)
Async XLA Ops:
  6.5 607.0 %copy-start = (bf16[3,640,640]{2,1,0:T(8,128)(2,1)S(1)}, bf16[3,640,640]{2,1,0:T(8,128)(2,1)}, u32[]{:S(2)}) copy-start(bf16[3,640,640]{2,1,0:T(8,128)(2,1)} %param.23) | copy-start | bytes 7372804
  6.5 178.9 %all-gather.4.cloned.1.call-start = ((), (), s32[]{:S(2)}) async-start(), calls=%async_computation.6 | async-start | bytes 3276800 | tf_op jit(solution)/shard_map/all_gather | solution.py:90
  133.9 258.6 %reduce-scatter.2.cloned.1.call-start = ((), (), s32[]{:S(2)}) async-start(), calls=%async_computation.5 | async-start | bytes 1228800 | tf_op jit(solution)/shard_map/reduce_scatter | solution.py:117
  190.0 3.3 copy-start.1
  228.3 4.5 copy-start.2
  331.3 8.7 %copy-start.3 = (bf16[80,12,64]{2,1,0:T(8,128)(2,1)S(1)}, bf16[80,12,64]{2,1,0:T(8,128)(2,1)}, u32[]{:S(2)}) copy-start(bf16[80,12,64]{2,1,0:T(8,128)(2,1)} %slice.94) | copy-start | bytes 368644
  453.4 4.5 copy-start.5
  453.4 4.5 copy-start.6
  453.4 76.9 %copy-start.7 = (f32[160]{0:T(256)S(1)}, f32[160]{0:T(256)}, u32[]{:S(2)}) copy-start(f32[160]{0:T(256)} %param.25) | copy-start | bytes 1924
  453.4 76.9 %copy-start.8 = (f32[160]{0:T(256)S(1)}, f32[160]{0:T(256)}, u32[]{:S(2)}) copy-start(f32[160]{0:T(256)} %param.24) | copy-start | bytes 1924
  537.8 18.4 %all-to-all-start.2 = ((bf16[32,2,1920]{2,1,0:T(2,128)(2,1)}), bf16[32,2,1920]{2,1,0:T(2,128)(2,1)S(1)}, u32[]{:S(2)}, u32[]{:S(2)}) async-start(bf16[32,2,1920]{2,1,0:T(2,128)(2,1)} %reshape.130), calls=%async_computation.3 | async-start | bytes 491520 | tf_op jit(solution)/shard_map/all_to_all | solution.py:88
  613.5 1.9 copy-start.4
Sparse Core Ops, SparseCore 0:
  134.0 51.3 all-gather.3
  350.6 41.9 reduce-scatter.1
where the time goes:
time: 656 us; the launch traced here: 647 us
  blocking collectives  288 us (44%)
  local copies, waits for them, and re-layouts  187 us (29%)
  waiting for transfers between devices  100 us (15%)
  other arithmetic  30.5 us (5%)
  matrix products  18.6 us (3%)
  between operations  13.9 us (2%)
  starting transfers between devices  7.99 us (1%)
    psum x2, blocking collectives, time_block(): sum_all, sum_sq = lax.psum((partial_sums[0], partial_sums[1]), 'frame')  147 us
    slice x9, local copies, waits for them, and re-layouts, columns(): padded[:, row_off:row_off + stride * out_rows:stride, col_off:col_off + s...  95.2 us
    all_gather x1, waiting for transfers between devices, time_block(): lax.all_gather(relaid, 'chan', axis=1, tiled=True)  51 us
    all_to_all x2, blocking collectives, time_block(): lax.all_to_all(mixed_out, 'frame', split_axis=0, concat_axis=2, tiled=True)  50.1 us
    all_gather x1, blocking collectives, time_block(): lax.all_gather(relaid, 'chan', axis=1, tiled=True)  47.8 us
    reduce_scatter x1, waiting for transfers between devices, per_device(): lax.psum_scatter(contract(flat_weight, stacked), 'chan', scatter_dimensio...  38 us
    unnamed x42, local copies, waits for them, and re-layouts  30.2 us
    unnamed x3, other arithmetic  23.3 us
  transfers between devices with their start and end apart: 3, of which 3 were waited for; matrix products, arithmetic and copies ran while one was open for 1% of the time, Pallas kernels for 0%

commit v1 on v0

v1 whole, which is shorter than its diff:
```python
import functools

import jax
import jax.numpy as jnp
from jax import lax
from jax.experimental import pallas as pl
from jax.experimental.pallas import tpu as pltpu
from jax.sharding import PartitionSpec as P

MESH = pl.DeviceIdType.MESH
BF = jnp.bfloat16
F32 = jnp.float32
C1 = 320
C2 = 640
GROUPS = 32
W1 = 128
H1 = 24
H2 = 12
W2 = 64
NX = 4
EPS = 1e-6

Q1 = C1 // 4
Q2 = C2 // 4
HALF1 = H1 * W1 // 2
WIN1 = HALF1 + W1
HALF2 = H2 * W2 // 2
POS2 = H2 * W2
DPAD = 768
DPART = DPAD // NX
CHUNKS = ((0, 128), (128, 512), (640, 512), (1152, 512))

SCRATCH = {
    "lat_v": ((Q1, H1 * W1), BF),
    "tw1_v": ((3 * C1, C1), BF),
    "tw2_v": ((3 * C2, C2), BF),
    "cw2_v": ((9 * C1, Q2), BF),
    "sw2_v": ((C1, Q2), BF),
    "raw1": ((3, 2, Q1, WIN1), BF),
    "hid1": ((2, 3, 2, Q1, WIN1), BF),
    "tmp1": ((C1, 6 * Q1), BF),
    "w1t": ((2, 2 * Q1, 6 * Q1), BF),
    "blk": ((2 * Q1, WIN1), BF),
    "dwt": ((2, DPAD, C1), BF),
    "taps1": ((2, 9 * Q1, HALF2), BF),
    "part": ((C1, HALF2), F32),
    "part_rx": ((C1 // 2, HALF2), F32),
    "red": ((2, 2, C1 // 2, HALF2), BF),
    "nrm": ((C1, POS2 + 256), BF),
    "taps2": ((10 * C1, POS2), BF),
    "w2t": ((Q2, 10 * C1), BF),
    "spat": ((Q2, POS2), BF),
    "raw2": ((3, 2, Q2, HALF2), BF),
    "hid2": ((2, 3, 2, Q2, HALF2), BF),
    "tmp2": ((C2, 6 * Q2), BF),
    "w4t": ((2, 2 * Q2, 6 * Q2), BF),
    "fin": ((2, Q2, HALF2), BF),
    "fin_rx": ((Q2, HALF2), BF),
    "par": ((2, 8, 256), F32),
    "par2": ((8, 384), F32),
    "st_tx": ((6, 1, 128), F32),
    "st_rx": ((32, 1, 128), F32),
}
N_SEM = 96


def dot(a, b):
    return lax.dot_general(a, b, (((1,), (0,)), ((), ())), preferred_element_type=F32)


def silu(u):
    return u / (1.0 + jnp.exp(-u))


def to_columns(rows):
    return jnp.concatenate([rows] * (128 // rows.shape[0]), axis=0).T


def one_hots(chan, size):
    lane = lax.broadcasted_iota(jnp.int32, (chan.shape[0], 128), 1) * size
    off = GROUPS * size
    first = (lane <= chan) & (chan < lane + size)
    second = (lane - off <= chan) & (chan < lane - off + size)
    return first, second


def group_row(sums, squares, chan, size):
    first, second = one_hots(chan, size)
    spread = jnp.where(first, sums, 0.0) + jnp.where(second, squares, 0.0)
    return jnp.sum(spread, axis=0, keepdims=True)


def scale_columns(row, count, chan, size, gain, shift):
    first, second = one_hots(chan, size)
    mean = jnp.sum(jnp.where(first, row, 0.0), axis=1, keepdims=True) / count
    square = jnp.sum(jnp.where(second, row, 0.0), axis=1, keepdims=True) / count
    scale = lax.rsqrt(square - mean * mean + EPS) * gain
    return scale, shift - mean * scale


def kernel(frames, *refs):
    (lat, tw1, g1, s1, dw, g2, s2, cw2, sw2, tb, tw2, g3, s3, out) = refs[:14]
    names = list(SCRATCH)
    r = dict(zip(names, refs[14 : 14 + len(names)]))
    send_sem, recv_sem, local_sem = refs[14 + len(names) :]
    ny = frames // NX
    f = lax.axis_index("frame")
    c = lax.axis_index("chan")
    x, y = f // ny, lax.rem(f, ny)
    zh, k = c // 2, lax.rem(c, 2)
    oz, ok = 1 - zh, 1 - k
    zp = {"chan": lax.rem(c + 2, 4)}
    kp = {"chan": c + 1 - 2 * k}
    after = {"frame": lax.rem(f + 1, frames)}
    before = {"frame": lax.rem(f + frames - 1, frames)}
    chan_peers = [{"chan": lax.rem(c + d, 4)} for d in range(1, 4)]
    x_peers = [{"frame": lax.rem(x + d, NX) * ny + y} for d in range(1, NX)]
    y_peers = [{"frame": x * ny + lax.rem(y + d, ny)} for d in range(1, ny)]

    loads = {}
    for number, (name, ref, dst) in enumerate(
        (
            ("lat", lat, r["lat_v"]),
            ("dw", dw, r["dwt"].at[zh, pl.ds(0, 9 * Q1)]),
            ("tw1", tw1, r["tw1_v"]),
            ("cw2", cw2, r["cw2_v"]),
            ("sw2", sw2, r["sw2_v"]),
            ("tw2", tw2, r["tw2_v"]),
        )
    ):
        loads[name] = pltpu.make_async_copy(ref, dst, local_sem.at[number])
        loads[name].start()

    barrier = pltpu.get_barrier_semaphore()
    greeted = chan_peers + x_peers + y_peers + [after, before]
    for peer in greeted:
        pl.semaphore_signal(barrier, inc=1, device_id=peer, device_id_type=MESH)

    counter = [0]
    sent = []

    def send(src, dst, peer):
        number = counter[0]
        counter[0] += 1
        copy = pltpu.make_async_remote_copy(
            src_ref=src,
            dst_ref=dst,
            send_sem=send_sem.at[number],
            recv_sem=recv_sem.at[number],
            device_id=peer,
            device_id_type=MESH,
        )
        copy.start()
        sent.append(copy)
        return copy

    def lanes(start, size):
        return pl.ds(pl.multiple_of(start, 128), size)

    st_tx, st_rx = r["st_tx"], r["st_rx"]
    stat_slot = [0, 0]

    def stat_send(row, peers):
        tx, rx = stat_slot
        stat_slot[0] += 1
        stat_slot[1] += len(peers)
        st_tx[tx] = row
        return [send(st_tx.at[tx], st_rx.at[rx + i], p) for i, p in enumerate(peers)], tx, rx

    def stat_wait(state):
        copies, tx, rx = state
        total = st_tx[tx]
        for i, copy in enumerate(copies):
            copy.wait_recv()
            total = total + st_rx[rx + i]
        return total

    raw1, raw2 = r["raw1"], r["raw2"]
    lat_v = r["lat_v"]

    par = r["par"]
    par[zh, 0:1, 0:Q1] = g1[...]
    par[zh, 1:2, 0:Q1] = s1[...]
    par[zh, 2:3, 0:Q2] = g3[...]
    par[zh, 3:4, 0:Q2] = s3[...]
    par[zh, 4:5, 0:Q2] = tb[...]
    r["par2"][0:1, 0:C1] = g2[...]
    r["par2"][1:2, 0:C1] = s2[...]
    loads["lat"].wait()
    raw1[1, zh, :, 0:W1] = lat_v[:, HALF1 - W1 : HALF1]
    raw1[1, zh, :, W1:WIN1] = lat_v[:, lanes(zh * HALF1, HALF1)]
    pl.semaphore_wait(barrier, len(greeted))

    z_copies = []
    for start, size in CHUNKS:
        if start == 0:
            src = lat_v.at[:, pl.ds(HALF1 - W1, W1)]
        else:
            src = lat_v.at[:, lanes(oz * HALF1 + start - W1, size)]
        z_copies.append(send(src, raw1.at[1, zh, :, pl.ds(start, size)], zp))
    y_own = [
        send(raw1.at[1, zh], raw1.at[0, zh], after),
        send(raw1.at[1, zh], raw1.at[2, zh], before),
    ]
    par_copy = send(par.at[zh], par.at[zh], zp)

    wide = lat_v[...].astype(F32)
    row_iota = lax.broadcasted_iota(jnp.int32, (Q1, 1), 0)
    row1 = group_row(
        jnp.sum(wide, axis=1, keepdims=True),
        jnp.sum(wide * wide, axis=1, keepdims=True),
        row_iota + c * Q1,
        C1 // GROUPS,
    )
    state = stat_send(row1, chan_peers)

    dwt = r["dwt"]
    loads["dw"].wait()
    dwt[zh, 9 * Q1 : DPAD, :] = jnp.zeros((DPAD - 9 * Q1, C1), BF)
    own_part = pl.ds(pl.multiple_of(x * DPART, DPART), DPART)
    dw_z = send(dwt.at[zh, own_part], dwt.at[zh, own_part], zp)

    loads["tw1"].wait()
    tmp1, w1t = r["tmp1"], r["w1t"]
    for slot, core in ((0, k), (1, ok)):
        rows = [
            r["tw1_v"][pl.ds(pl.multiple_of(t * C1 + z * 2 * Q1 + core * Q1, 16), Q1), :]
            for t in range(3)
            for z in range(2)
        ]
        tmp1[...] = jnp.concatenate(rows, axis=0).T
        for z in range(2):
            w1t[slot, z * Q1 : (z + 1) * Q1, :] = tmp1[
                pl.ds(pl.multiple_of(z * 2 * Q1 + k * Q1, 16), Q1), :
            ]

    state = stat_send(stat_wait(state), x_peers)

    y_fwd = []

    def forward(index):
        start, size = CHUNKS[index]
        z_copies[index].wait_recv()
        here = raw1.at[1, oz, :, pl.ds(start, size)]
        y_fwd.append(send(here, raw1.at[0, oz, :, pl.ds(start, size)], after))
        y_fwd.append(send(here, raw1.at[2, oz, :, pl.ds(start, size)], before))

    forward(0)
    state = stat_send(stat_wait(state), y_peers)
    forward(1)
    w2t = r["w2t"]
    loads["cw2"].wait()
    loads["sw2"].wait()
    for t in range(9):
        w2t[:, t * C1 : (t + 1) * C1] = r["cw2_v"][t * C1 : (t + 1) * C1, :].T
    w2t[:, 9 * C1 : 10 * C1] = r["sw2_v"][...].T
    forward(2)
    tmp2, w4t = r["tmp2"], r["w4t"]
    loads["tw2"].wait()

    def prepare(slot, core):
        rows = [
            r["tw2_v"][pl.ds(pl.multiple_of(t * C2 + z * 2 * Q2 + core * Q2, 16), Q2), :]
            for t in range(3)
            for z in range(2)
        ]
        tmp2[...] = jnp.concatenate(rows, axis=0).T
        for z in range(2):
            w4t[slot, z * Q2 : (z + 1) * Q2, :] = tmp2[
                pl.ds(pl.multiple_of(z * 2 * Q2 + k * Q2, 16), Q2), :
            ]

    prepare(0, k)
    forward(3)
    prepare(1, ok)
    dw_z.wait_recv()
    other_part = dwt.at[oz, own_part]
    dw_x = [send(other_part, other_part, p) for p in x_peers]

    par_copy.wait_recv()
    cols = [to_columns(par[z]) for z in range(2)]
    total = stat_wait(state)
    row_iota = lax.broadcasted_iota(jnp.int32, (Q1, 1), 0)
    affine1 = [
        scale_columns(
            total,
            float(C1 // GROUPS * H1 * W1 * frames),
            row_iota + (2 * z + k) * Q1,
            C1 // GROUPS,
            cols[z][0:Q1, 0:1],
            cols[z][0:Q1, 1:2],
        )
        for z in range(2)
    ]
    hid1 = r["hid1"]
    alive = {0: f > 0, 2: f < frames - 1}

    def pick(pair, z):
        return [jnp.where(z == 0, pair[0][i], pair[1][i]) for i in range(2)]

    def hidden(raw, hid, tap, z, affine):
        scale, shift = pick(affine, z)
        value = silu(raw[tap, z].astype(F32) * scale + shift)
        if tap != 1:
            value = jnp.where(alive[tap], value, 0.0)
        hid[0, tap, z] = value.astype(BF)
        return send(hid.at[0, tap, z], hid.at[1, tap, z], kp)

    k_copies = [hidden(raw1, hid1, 1, zh, affine1)]
    for tap, copy in ((0, y_own[0]), (2, y_own[1])):
        copy.wait_recv()
        k_copies.append(hidden(raw1, hid1, tap, zh, affine1))
    k_copies.append(hidden(raw1, hid1, 1, oz, affine1))
    for tap in (0, 2):
        for copy in y_fwd[tap // 2 :: 2]:
            copy.wait_recv()
        k_copies.append(hidden(raw1, hid1, tap, oz, affine1))
    for copy in k_copies:
        copy.wait_recv()

    blk = r["blk"]
    for start, size in CHUNKS:
        span = slice(start, start + size)
        mixed = sum(
            dot(w1t[slot], hid1[slot, :, :, :, span].reshape(6 * Q1, size)) for slot in range(2)
        ).astype(BF)
        value = raw1[1, :, :, span].reshape(2 * Q1, size).astype(F32) + mixed.astype(F32)
        if start == 0:
            value = jnp.where(zh == 0, 0.0, value)
        blk[:, span] = value.astype(BF)

    src = lax.broadcasted_iota(jnp.int32, (256, 128), 0)
    dst = lax.broadcasted_iota(jnp.int32, (256, 128), 1)
    same = (src >= 128) == (dst >= 64)
    src_col = src - jnp.where(src >= 128, 128, 0)
    dst_col = dst - jnp.where(dst >= 64, 64, 0)
    taps1 = r["taps1"]
    picks = jnp.concatenate(
        [
            jnp.where(same & (src_col == 2 * dst_col + dx - 1), 1.0, 0.0).astype(BF)
            for dx in range(3)
        ],
        axis=1,
    )
    for dy in range(3):
        for j in range(HALF2 // 128):
            top = (4 * j + dy) * W1
            pair = jnp.concatenate(
                [blk[:, top : top + W1], blk[:, top + 2 * W1 : top + 3 * W1]], axis=1
            )
            got = dot(pair, picks).astype(BF)
            for dx in range(3):
                t = 3 * dy + dx
                for z in range(2):
                    taps1[z, t * Q1 : (t + 1) * Q1, j * 128 : (j + 1) * 128] = got[
                        z * Q1 : (z + 1) * Q1, dx * 128 : (dx + 1) * 128
                    ]
    for copy in dw_x:
        copy.wait_recv()
    part = r["part"]
    part[...] = sum(
        lax.dot_general(
            dwt[z, 0 : 9 * Q1, :],
            taps1[z],
            (((0,), (0,)), ((), ())),
            preferred_element_type=F32,
        )
        for z in range(2)
    )
    half = C1 // 2
    part_copy = send(
        part.at[pl.ds(pl.multiple_of(ok * half, 16), half)], r["part_rx"], kp
    )
    part_copy.wait_recv()
    red = r["red"]
    mine = part[pl.ds(pl.multiple_of(k * half, 16), half), :]
    red[k, zh] = (mine + r["part_rx"][...]).astype(BF)
    red_z = send(red.at[k, zh], red.at[k, zh], zp)
    red_k = send(red.at[k, zh], red.at[k, zh], kp)
    red_z.wait_recv()
    red_k2 = send(red.at[k, oz], red.at[k, oz], kp)
    red_k.wait_recv()
    red_k2.wait_recv()

    nrm, taps2 = r["nrm"], r["taps2"]
    nrm[:, 0:128] = jnp.zeros((C1, 128), BF)
    nrm[:, 128 + POS2 :] = jnp.zeros((C1, 128), BF)
    cols2 = to_columns(r["par2"][...])
    half_iota = lax.broadcasted_iota(jnp.int32, (half, 1), 0)
    for core in range(2):
        pieces = [red[core, z] for z in range(2)]
        wide = jnp.concatenate(pieces, axis=1).astype(F32)
        chan = half_iota + core * half
        row2 = group_row(
            jnp.sum(wide, axis=1, keepdims=True),
            jnp.sum(wide * wide, axis=1, keepdims=True),
            chan,
            C1 // GROUPS,
        )
        span = slice(core * half, (core + 1) * half)
        scale, shift = scale_columns(
            row2, float(C1 // GROUPS * POS2), chan, C1 // GROUPS, cols2[span, 0:1], cols2[span, 1:2]
        )
        nrm[span, 128 : 128 + POS2] = silu(wide * scale + shift).astype(BF)
        for z in range(2):
            taps2[9 * C1 + core * half : 9 * C1 + (core + 1) * half, z * HALF2 : (z + 1) * HALF2] = (
                pieces[z]
            )

    src = lax.broadcasted_iota(jnp.int32, (256, 256), 0)
    dst = lax.broadcasted_iota(jnp.int32, (256, 256), 1)
    second = dst >= 128
    lane = dst - jnp.where(second, 128, 0)
    upper = lane >= 64
    col = lane - jnp.where(upper, 64, 0)
    base = jnp.where(second, 128, 64) + jnp.where(upper, 64, 0)
    for dx in range(3):
        want = col + (dx - 1)
        keep = (want >= 0) & (want < W2) & (src == base + want)
        pick2 = jnp.where(keep, 1.0, 0.0).astype(BF)
        for j in range(POS2 // 128 + 1):
            got = dot(nrm[:, j * 128 : j * 128 + 256], pick2).astype(BF)
            if j < POS2 // 128:
                at = slice(j * 128, (j + 1) * 128)
                taps2[dx * C1 : (dx + 1) * C1, at] = got[:, 0:128]
                taps2[(3 + dx) * C1 : (4 + dx) * C1, at] = got[:, 128:256]
            if j > 0:
                at = slice((j - 1) * 128, j * 128)
                taps2[(6 + dx) * C1 : (7 + dx) * C1, at] = got[:, 0:128]
    spat = r["spat"]
    bias = jnp.where(zh == 0, cols[0][0:Q2, 4:5], cols[1][0:Q2, 4:5])
    for j in range(POS2 // 256):
        at = slice(j * 256, (j + 1) * 256)
        spat[:, at] = (dot(w2t[...], taps2[:, at]) + bias).astype(BF)

    raw2[1, zh] = spat[:, lanes(zh * HALF2, HALF2)]
    z2 = send(spat.at[:, lanes(oz * HALF2, HALF2)], raw2.at[1, zh], zp)
    y2_own = [
        send(raw2.at[1, zh], raw2.at[0, zh], after),
        send(raw2.at[1, zh], raw2.at[2, zh], before),
    ]
    wide = spat[...].astype(F32)
    row_iota = lax.broadcasted_iota(jnp.int32, (Q2, 1), 0)
    row3 = group_row(
        jnp.sum(wide, axis=1, keepdims=True),
        jnp.sum(wide * wide, axis=1, keepdims=True),
        row_iota + c * Q2,
        C2 // GROUPS,
    )
    state = stat_send(row3, chan_peers)
    state = stat_send(stat_wait(state), x_peers)
    z2.wait_recv()
    y2_fwd = [
        send(raw2.at[1, oz], raw2.at[0, oz], after),
        send(raw2.at[1, oz], raw2.at[2, oz], before),
    ]
    state = stat_send(stat_wait(state), y_peers)
    total = stat_wait(state)
    affine3 = [
        scale_columns(
            total,
            float(C2 // GROUPS * POS2 * frames),
            row_iota + (2 * z + k) * Q2,
            C2 // GROUPS,
            cols[z][0:Q2, 2:3],
            cols[z][0:Q2, 3:4],
        )
        for z in range(2)
    ]
    hid2 = r["hid2"]
    k2_copies = [hidden(raw2, hid2, 1, zh, affine3), hidden(raw2, hid2, 1, oz, affine3)]
    for z, copies in ((zh, y2_own), (oz, y2_fwd)):
        for tap in (0, 2):
            copies[tap // 2].wait_recv()
            k2_copies.append(hidden(raw2, hid2, tap, z, affine3))
    for copy in k2_copies:
        copy.wait_recv()
    fin = r["fin"]
    mixed = sum(
        dot(w4t[slot], hid2[slot].reshape(6 * Q2, HALF2)) for slot in range(2)
    ).astype(BF)
    value = raw2[1].reshape(2 * Q2, HALF2).astype(F32) + mixed.astype(F32)
    fin[...] = value.astype(BF).reshape(2, Q2, HALF2)
    last = send(fin.at[oz], r["fin_rx"], zp)
    out[:, lanes(zh * HALF2, HALF2)] = fin[zh]
    last.wait_recv()
    out[:, lanes(oz * HALF2, HALF2)] = r["fin_rx"][...]
    for copy in sent:
        copy.wait_send()


def per_device(frames, lat, tw1, g1, s1, dw, g2, s2, cw2, sw2, tb, tw2, g3, s3):
    vmem = pl.BlockSpec(memory_space=pltpu.VMEM)
    far = pl.BlockSpec(memory_space=pl.ANY)
    row = lambda v: v.reshape(1, v.shape[0])
    result = pl.pallas_call(
        functools.partial(kernel, frames),
        out_shape=jax.ShapeDtypeStruct((Q2, POS2), BF),
        in_specs=[far, far, vmem, vmem, far, vmem, vmem, far, far, vmem, far, vmem, vmem],
        out_specs=vmem,
        scratch_shapes=[pltpu.VMEM(shape, dtype) for shape, dtype in SCRATCH.values()]
        + [
            pltpu.SemaphoreType.DMA((N_SEM,)),
            pltpu.SemaphoreType.DMA((N_SEM,)),
            pltpu.SemaphoreType.DMA((8,)),
        ],
        compiler_params=pltpu.CompilerParams(
            collective_id=0, has_side_effects=True, vmem_limit_bytes=56 * 2**20
        ),
        name="video_block",
    )(
        lat.reshape(Q1, H1 * W1),
        tw1.reshape(3 * C1, C1),
        row(g1),
        row(s1),
        dw.reshape(9 * Q1, C1),
        row(g2),
        row(s2),
        cw2.reshape(9 * C1, Q2),
        sw2,
        row(tb),
        tw2.reshape(3 * C2, C2),
        row(g3),
        row(s3),
    )
    return result.reshape(1, Q2, POS2)


def solution(mesh):
    return jax.shard_map(
        functools.partial(per_device, mesh.shape["frame"]),
        mesh=mesh,
        in_specs=(
            P(("video", "frame"), "chan", None),
            P(),
            P("chan"),
            P("chan"),
            P(None, "chan", None),
            P(),
            P(),
            P(None, None, "chan"),
            P(None, "chan"),
            P("chan"),
            P(),
            P("chan"),
            P("chan"),
        ),
        out_specs=P(("video", "frame"), "chan", None),
        check_vma=False,
    )
```

time: 656 us -> 97.8 us (0.15)
  the two profiles are of different devices: /device:TPU:8 before, /device:TPU:65 now
where the time goes in v1:
time: 97.8 us; the launch traced here: 97.5 us
  Pallas kernels  89.1 us (91%)
  local copies, waits for them, and re-layouts  8.46 us (9%)
    pallas_call x1, Pallas kernels, per_device(): pl.pallas_call(functools.partial(kernel, frames), out_shape=jax.ShapeDtyp...  89.1 us
    unnamed x3, local copies, waits for them, and re-layouts  5.93 us
    reshape x2, local copies, waits for them, and re-layouts, per_device(): row = lambda v: v.reshape(1, v.shape[0])  2.53 us

profile of v1, /device:TPU:65, one launch (start us, length us, event | category | flops | bytes accessed | tf_op | source)
XLA Modules:
  0.0 97.5 jit_solution(15418238100267515314)
XLA Ops:
  0.0 1.3 %reshape.44.refs_5_ = f32[1,320]{1,0:T(1,128)} reshape(f32[320]{0:T(512)} %param.18) | data formatting | bytes 2560 | tf_op jit(solution)/shard_map/reshape | solution.py:495
  1.3 1.3 %reshape.45.refs_6_ = f32[1,320]{1,0:T(1,128)} reshape(f32[320]{0:T(512)} %param.19) | data formatting | bytes 2560 | tf_op jit(solution)/shard_map/reshape | solution.py:495
  2.5 1.7 %copy.15.refs_8_ = bf16[320,160]{1,0:T(8,128)(2,1)} copy(bf16[320,160]{0,1:T(8,128)(2,1)} %param.21) | data formatting | bytes 204800 | tf_op args[8]
  4.2 2.6 %copy.14 = bf16[9,320,160]{2,1,0:T(8,128)(2,1)} copy(bf16[9,320,160]{1,2,0:T(8,128)(2,1)} %param.20) | data formatting | bytes 1843200 | tf_op args[7]
  6.8 89.1 %video_block.1 = bf16[160,768]{1,0:T(8,128)(2,1)} custom-call(bf16[80,3072]{1,0:T(8,128)(2,1)} %bitcast.16, bf16[960,320]{1,0:T(8,128)(2,1)} %bitcast.14, f32[1,80]{1,0:T(1,128)} %bitcast.20, f32[1,80]{1,0:T(1,128)} %bitcast.21, bf16[720,320]{1,0:T(8,128)(2,1)} %bitcast.15, f32[1,320]{1,0:T(1,128)} %reshape.44.refs_5_, f32[1,320]{1,0:T(1,128)} %reshape.45.refs_6_, ...), custom_call_target="tpu_custom_call" | custom-call | tf_op jit(solution)/shard_map/video_block/pallas_call | solution.py:496
  95.9 1.7 %copy.17 = bf16[1,160,768]{2,1,0:T(8,128)(2,1)} copy(bf16[1,160,768]{2,1,0:T(8,128)(2,1)} %bitcast.13) | data formatting | bytes 491520

commit v2 on v1

v2 whole, which is shorter than its diff:
```python
import functools

import jax
import jax.numpy as jnp
from jax import lax
from jax.experimental import pallas as pl
from jax.experimental.pallas import tpu as pltpu
from jax.sharding import PartitionSpec as P

MESH = pl.DeviceIdType.MESH
BF = jnp.bfloat16
F32 = jnp.float32
C1 = 320
C2 = 640
GROUPS = 32
W1 = 128
H1 = 24
H2 = 12
W2 = 64
NX = 4
EPS = 1e-6

Q1 = C1 // 4
Q2 = C2 // 4
HALF1 = H1 * W1 // 2
WIN1 = HALF1 + W1
HALF2 = H2 * W2 // 2
POS2 = H2 * W2
DPAD = 768
DPART = DPAD // NX
TILES = HALF2 // 128
CHUNKS = ((0, 640), (640, 512), (1152, 512))

SCRATCH = {
    "lat_v": ((Q1, H1 * W1), BF),
    "tw1_v": ((3 * C1, C1), BF),
    "tw2_v": ((3 * C2, C2), BF),
    "cw2_v": ((9 * Q2, C1), BF),
    "sw2_v": ((Q2, C1), BF),
    "zsrc": ((Q1, WIN1), BF),
    "raw1": ((3, 2, Q1, WIN1), BF),
    "hid1": ((2, 3, 2, Q1, WIN1), BF),
    "tmp1": ((C1, 6 * Q1), BF),
    "w1t": ((2, 2 * Q1, 6 * Q1), BF),
    "blk": ((2 * Q1, WIN1), BF),
    "dwt": ((2, DPAD, C1), BF),
    "taps1": ((2, 9 * Q1, HALF2), BF),
    "part": ((C1, HALF2), F32),
    "part_rx": ((C1 // 2, HALF2), F32),
    "red": ((2, 2, C1 // 2, HALF2), BF),
    "nrm": ((C1, POS2 + 256), BF),
    "taps2": ((10 * C1, POS2), BF),
    "w2t": ((Q2, 10 * C1), BF),
    "spat": ((Q2, POS2), BF),
    "raw2": ((3, 2, Q2, HALF2), BF),
    "hid2": ((2, 3, 2, Q2, HALF2), BF),
    "tmp2": ((C2, 6 * Q2), BF),
    "w4t": ((2, 2, Q2, 6 * Q2), BF),
    "pick1": ((256, 384), BF),
    "pick2": ((3, 256, 256), BF),
    "fin": ((Q2, HALF2), BF),
    "fin_rx": ((Q2, HALF2), BF),
    "par": ((2, 8, 256), F32),
    "par2": ((8, 384), F32),
    "st_tx": ((6, 1, 128), F32),
    "st_rx": ((32, 1, 128), F32),
}
N_SEM = 128


def dot(a, b):
    return lax.dot_general(a, b, (((1,), (0,)), ((), ())), preferred_element_type=F32)


def silu_of_half(w):
    return w + w * jnp.tanh(w)


def to_columns(rows):
    return jnp.concatenate([rows] * (128 // rows.shape[0]), axis=0).T


def one_hots(chan, size):
    lane = lax.broadcasted_iota(jnp.int32, (chan.shape[0], 128), 1) * size
    off = GROUPS * size
    first = (lane <= chan) & (chan < lane + size)
    second = (lane - off <= chan) & (chan < lane - off + size)
    return first, second


def group_row(sums, squares, chan, size):
    first, second = one_hots(chan, size)
    spread = jnp.where(first, sums, 0.0) + jnp.where(second, squares, 0.0)
    return jnp.sum(spread, axis=0, keepdims=True)


def scale_columns(row, count, chan, size, gain, shift):
    first, second = one_hots(chan, size)
    mean = jnp.sum(jnp.where(first, row, 0.0), axis=1, keepdims=True) / count
    square = jnp.sum(jnp.where(second, row, 0.0), axis=1, keepdims=True) / count
    scale = lax.rsqrt(square - mean * mean + EPS) * gain
    return 0.5 * scale, 0.5 * (shift - mean * scale)


class Done:
    def wait_recv(self):
        pass


def kernel(frames, *refs):
    (lat, tw1, g1, s1, dw, g2, s2, cw2, sw2, tb, tw2, g3, s3, out) = refs[:14]
    names = list(SCRATCH)
    r = dict(zip(names, refs[14 : 14 + len(names)]))
    send_sem, recv_sem, local_sem = refs[14 + len(names) :]
    ny = frames // NX
    f = lax.axis_index("frame")
    c = lax.axis_index("chan")
    x, y = f // ny, lax.rem(f, ny)
    zh, k = c // 2, lax.rem(c, 2)
    oz, ok = 1 - zh, 1 - k
    zp = {"chan": lax.rem(c + 2, 4)}
    kp = {"chan": c + 1 - 2 * k}
    after = {"frame": lax.rem(f + 1, frames)}
    before = {"frame": lax.rem(f + frames - 1, frames)}
    chan_peers = [{"chan": lax.rem(c + d, 4)} for d in range(1, 4)]
    x_peers = [{"frame": lax.rem(x + d, NX) * ny + y} for d in range(1, NX)]
    y_peers = [{"frame": x * ny + lax.rem(y + d, ny)} for d in range(1, ny)]

    loads = {}
    for number, (name, ref, dst) in enumerate(
        (
            ("lat", lat, r["lat_v"]),
            ("dw", dw, r["dwt"].at[zh, pl.ds(0, 9 * Q1)]),
            ("tw1", tw1, r["tw1_v"]),
            ("cw2", cw2, r["cw2_v"]),
            ("sw2", sw2, r["sw2_v"]),
            ("tw2", tw2, r["tw2_v"]),
        )
    ):
        loads[name] = pltpu.make_async_copy(ref, dst, local_sem.at[number])
        loads[name].start()

    barrier = pltpu.get_barrier_semaphore()
    greeted = chan_peers + x_peers + y_peers + [after, before]
    for peer in greeted:
        pl.semaphore_signal(barrier, inc=1, device_id=peer, device_id_type=MESH)

    counter = [0]
    sent = []

    def send(src, dst, peer):
        number = counter[0]
        counter[0] += 1
        copy = pltpu.make_async_remote_copy(
            src_ref=src,
            dst_ref=dst,
            send_sem=send_sem.at[number],
            recv_sem=recv_sem.at[number],
            device_id=peer,
            device_id_type=MESH,
        )
        copy.start()
        sent.append(copy)
        return copy

    def lanes(start, size):
        return pl.ds(pl.multiple_of(start, 128), size)

    st_tx, st_rx = r["st_tx"], r["st_rx"]
    stat_slot = [0, 0]

    def stat_send(row, peers):
        tx, rx = stat_slot
        stat_slot[0] += 1
        stat_slot[1] += len(peers)
        st_tx[tx] = row
        return [send(st_tx.at[tx], st_rx.at[rx + i], p) for i, p in enumerate(peers)], tx, rx

    def stat_wait(state):
        copies, tx, rx = state
        total = st_tx[tx]
        for i, copy in enumerate(copies):
            copy.wait_recv()
            total = total + st_rx[rx + i]
        return total

    raw1, raw2 = r["raw1"], r["raw2"]
    lat_v = r["lat_v"]

    par = r["par"]
    par[zh, 0:1, 0:Q1] = g1[...]
    par[zh, 1:2, 0:Q1] = s1[...]
    par[zh, 2:3, 0:Q2] = g3[...]
    par[zh, 3:4, 0:Q2] = s3[...]
    par[zh, 4:5, 0:Q2] = tb[...]
    r["par2"][0:1, 0:C1] = g2[...].reshape(1, C1)
    r["par2"][1:2, 0:C1] = s2[...].reshape(1, C1)
    loads["lat"].wait()
    zsrc = r["zsrc"]
    raw1[1, zh, :, 0:W1] = lat_v[:, HALF1 - W1 : HALF1]
    raw1[1, zh, :, W1:WIN1] = lat_v[:, lanes(zh * HALF1, HALF1)]
    zsrc[:, 0:W1] = lat_v[:, HALF1 - W1 : HALF1]
    zsrc[:, W1:WIN1] = lat_v[:, lanes(oz * HALF1, HALF1)]
    wide = lat_v[...].astype(F32)
    q1_iota = lax.broadcasted_iota(jnp.int32, (Q1, 1), 0)
    row1 = group_row(
        jnp.sum(wide, axis=1, keepdims=True),
        jnp.sum(wide * wide, axis=1, keepdims=True),
        q1_iota + c * Q1,
        C1 // GROUPS,
    )
    dwt = r["dwt"]
    loads["dw"].wait()
    dwt[zh, 9 * Q1 : DPAD, :] = jnp.zeros((DPAD - 9 * Q1, C1), BF)
    pl.semaphore_wait(barrier, len(greeted))

    state = stat_send(row1, chan_peers)
    pieces = ny // 2
    piece = DPART // pieces
    own_piece = pl.ds(pl.multiple_of(x * DPART + (y // 2) * piece, 16), piece)
    own_part = pl.ds(pl.multiple_of(x * DPART, 16), DPART)
    dw_z = send(dwt.at[zh, own_piece], dwt.at[zh, own_piece], zp)

    z_copies = [
        send(zsrc.at[:, pl.ds(a, n)], raw1.at[1, zh, :, pl.ds(a, n)], zp) for a, n in CHUNKS
    ]

    def to_frames(raw, z, a, n):
        here = raw.at[1, z, :, pl.ds(a, n)]
        return [
            send(here, raw.at[0, z, :, pl.ds(a, n)], after),
            send(here, raw.at[2, z, :, pl.ds(a, n)], before),
        ]

    y_own = [to_frames(raw1, zh, a, n) for a, n in CHUNKS]
    par_copy = send(par.at[zh], par.at[zh], zp)

    def prepare(weight, held, store, width, count, slot, core):
        rows = [
            weight[pl.ds(pl.multiple_of(t * width + z * 2 * count + core * count, 16), count), :]
            for t in range(3)
            for z in range(2)
        ]
        held[...] = jnp.concatenate(rows, axis=0).T
        for z in range(2):
            store(slot, z, held[pl.ds(pl.multiple_of(z * 2 * count + k * count, 16), count), :])

    w1t, w4t, w2t = r["w1t"], r["w4t"], r["w2t"]

    def store1(slot, z, value):
        w1t[slot, z * Q1 : (z + 1) * Q1, :] = value

    def store4(slot, z, value):
        w4t[slot, z] = value

    loads["tw1"].wait()
    for slot, core in ((0, k), (1, ok)):
        prepare(r["tw1_v"], r["tmp1"], store1, C1, Q1, slot, core)

    src = lax.broadcasted_iota(jnp.int32, (256, 128), 0)
    dst = lax.broadcasted_iota(jnp.int32, (256, 128), 1)
    same = (src >= 128) == (dst >= 64)
    src_col = src - jnp.where(src >= 128, 128, 0)
    dst_col = dst - jnp.where(dst >= 64, 64, 0)
    for dx in range(3):
        r["pick1"][:, dx * 128 : (dx + 1) * 128] = jnp.where(
            same & (src_col == 2 * dst_col + dx - 1), 1.0, 0.0
        ).astype(BF)

    state = stat_send(stat_wait(state), x_peers)
    dw_z.wait_recv()
    here = dwt.at[oz, own_piece]
    dw_y = [
        send(here, here, {"frame": x * ny + lax.rem(y + 2 * d, ny)}) for d in range(1, pieces)
    ]

    src = lax.broadcasted_iota(jnp.int32, (256, 256), 0)
    dst = lax.broadcasted_iota(jnp.int32, (256, 256), 1)
    second = dst >= 128
    lane = dst - jnp.where(second, 128, 0)
    upper = lane >= 64
    col = lane - jnp.where(upper, 64, 0)
    base = jnp.where(second, 128, 64) + jnp.where(upper, 64, 0)
    for dx in range(3):
        want = col + (dx - 1)
        keep = (want >= 0) & (want < W2) & (src == base + want)
        r["pick2"][dx] = jnp.where(keep, 1.0, 0.0).astype(BF)
    loads["cw2"].wait()
    loads["sw2"].wait()
    for t in range(9):
        w2t[:, t * C1 : (t + 1) * C1] = r["cw2_v"][t * Q2 : (t + 1) * Q2, :]
    w2t[:, 9 * C1 : 10 * C1] = r["sw2_v"][...]
    state = stat_send(stat_wait(state), y_peers)
    y_fwd = []

    def forward(i):
        z_copies[i].wait_recv()
        y_fwd.append(to_frames(raw1, oz, *CHUNKS[i]))

    forward(0)
    loads["tw2"].wait()
    for slot, core in ((0, k), (1, ok)):
        prepare(r["tw2_v"], r["tmp2"], store4, C2, Q2, slot, core)
    par_copy.wait_recv()
    cols = [to_columns(par[z]) for z in range(2)]
    cols2 = to_columns(r["par2"][...])
    bias = jnp.where(zh == 0, cols[0][0:Q2, 4:5], cols[1][0:Q2, 4:5])
    total = stat_wait(state)
    affine1 = [
        scale_columns(
            total,
            float(C1 // GROUPS * H1 * W1 * frames),
            q1_iota + (2 * z + k) * Q1,
            C1 // GROUPS,
            cols[z][0:Q1, 0:1],
            cols[z][0:Q1, 1:2],
        )
        for z in range(2)
    ]
    for copy in dw_y:
        copy.wait_recv()
    other_part = dwt.at[oz, own_part]
    dw_x = [send(other_part, other_part, p) for p in x_peers]
    forward(1)
    hid1 = r["hid1"]
    alive = {0: f > 0, 2: f < frames - 1}

    def pick(pair, z):
        return [jnp.where(z == 0, pair[0][i], pair[1][i]) for i in range(2)]

    def hidden(raw, hid, z, affine, a, n, waits):
        span = slice(a, a + n)
        scale, shift = pick(affine, z)
        for tap in (1, 0, 2):
            if tap != 1:
                waits[tap // 2].wait_recv()
            value = silu_of_half(raw[tap, z, :, span].astype(F32) * scale + shift)
            if tap != 1:
                value = jnp.where(alive[tap], value, 0.0)
            hid[0, tap, z, :, span] = value.astype(BF)
        return send(hid.at[0, :, z, :, pl.ds(a, n)], hid.at[1, :, z, :, pl.ds(a, n)], kp)

    blk, taps1 = r["blk"], r["taps1"]
    part, part_rx, red = r["part"], r["part_rx"], r["red"]
    half = C1 // 2
    k1, part_k, red_z, red_k = {}, {}, {}, {}

    def hid_own(i):
        k1[i] = [hidden(raw1, hid1, zh, affine1, *CHUNKS[i], y_own[i])]

    def hid_other(i):
        k1[i].append(hidden(raw1, hid1, oz, affine1, *CHUNKS[i], y_fwd[i]))

    def first_conv(i):
        a, n = CHUNKS[i]
        span = slice(a, a + n)
        for copy in k1[i]:
            copy.wait_recv()
        mixed = sum(
            dot(w1t[slot], hid1[slot, :, :, :, span].reshape(6 * Q1, n)) for slot in range(2)
        ).astype(BF)
        value = raw1[1, :, :, span].reshape(2 * Q1, n).astype(F32) + mixed.astype(F32)
        if i == 0:
            blk[:, 0:W1] = jnp.where(zh == 0, 0.0, value[:, 0:W1]).astype(BF)
            blk[:, W1:n] = value[:, W1:].astype(BF)
        else:
            blk[:, span] = value.astype(BF)
        at = slice(i * 128, (i + 1) * 128)
        for dy in range(3):
            top = (4 * i + dy) * W1
            pair = jnp.concatenate(
                [blk[:, top : top + W1], blk[:, top + 2 * W1 : top + 3 * W1]], axis=1
            )
            got = dot(pair, r["pick1"][...]).astype(BF)
            for dx in range(3):
                t = 3 * dy + dx
                for z in range(2):
                    taps1[z, t * Q1 : (t + 1) * Q1, at] = got[
                        z * Q1 : (z + 1) * Q1, dx * 128 : (dx + 1) * 128
                    ]

    def down(i):
        at = slice(i * 128, (i + 1) * 128)
        part[:, at] = sum(
            lax.dot_general(
                dwt[z, 0 : 9 * Q1, :],
                taps1[z, :, at],
                (((0,), (0,)), ((), ())),
                preferred_element_type=F32,
            )
            for z in range(2)
        )
        part_k[i] = send(
            part.at[pl.ds(pl.multiple_of(ok * half, 16), half), pl.ds(i * 128, 128)],
            part_rx.at[:, pl.ds(i * 128, 128)],
            kp,
        )

    def reduced(i):
        at = slice(i * 128, (i + 1) * 128)
        part_k[i].wait_recv()
        mine = part[pl.ds(pl.multiple_of(k * half, 16), half), at]
        red[k, zh, :, at] = (mine + part_rx[:, at]).astype(BF)
        here = red.at[k, zh, :, pl.ds(i * 128, 128)]
        red_z[i] = send(here, here, zp)
        red_k[i] = [send(here, here, kp)]

    def pass_reduced(i):
        red_z[i].wait_recv()
        here = red.at[k, oz, :, pl.ds(i * 128, 128)]
        red_k[i].append(send(here, here, kp))

    hid_own(0)
    hid_other(0)
    hid_own(1)
    hid_other(1)
    first_conv(0)
    forward(2)
    first_conv(1)
    hid_own(2)
    for copy in dw_x:
        copy.wait_recv()
    down(0)
    down(1)
    hid_other(2)
    reduced(0)
    reduced(1)
    first_conv(2)
    down(2)
    reduced(2)
    for i in range(3):
        pass_reduced(i)
    for i in range(3):
        for copy in red_k[i]:
            copy.wait_recv()

    nrm, taps2 = r["nrm"], r["taps2"]
    nrm[:, 0:128] = jnp.zeros((C1, 128), BF)
    nrm[:, 128 + POS2 :] = jnp.zeros((C1, 128), BF)
    half_iota = lax.broadcasted_iota(jnp.int32, (half, 1), 0)
    for core in range(2):
        sides = [red[core, z] for z in range(2)]
        wide = jnp.concatenate(sides, axis=1).astype(F32)
        chan = half_iota + core * half
        row2 = group_row(
            jnp.sum(wide, axis=1, keepdims=True),
            jnp.sum(wide * wide, axis=1, keepdims=True),
            chan,
            C1 // GROUPS,
        )
        span = slice(core * half, (core + 1) * half)
        scale, shift = scale_columns(
            row2, float(C1 // GROUPS * POS2), chan, C1 // GROUPS, cols2[span, 0:1], cols2[span, 1:2]
        )
        nrm[span, 128 : 128 + POS2] = silu_of_half(wide * scale + shift).astype(BF)
        for z in range(2):
            taps2[9 * C1 + core * half : 9 * C1 + (core + 1) * half, z * HALF2 : (z + 1) * HALF2] = (
                sides[z]
            )

    for dx in range(3):
        for j in range(POS2 // 128 + 1):
            got = dot(nrm[:, j * 128 : j * 128 + 256], r["pick2"][dx]).astype(BF)
            if j < POS2 // 128:
                at = slice(j * 128, (j + 1) * 128)
                taps2[dx * C1 : (dx + 1) * C1, at] = got[:, 0:128]
                taps2[(3 + dx) * C1 : (4 + dx) * C1, at] = got[:, 128:256]
            if j > 0:
                at = slice((j - 1) * 128, j * 128)
                taps2[(6 + dx) * C1 : (7 + dx) * C1, at] = got[:, 0:128]

    spat = r["spat"]
    z2 = []
    for i in range(TILES):
        at = lanes(oz * HALF2 + i * 128, 128)
        spat[:, at] = (dot(w2t[...], taps2[:, at]) + bias).astype(BF)
        z2.append(send(spat.at[:, at], raw2.at[1, zh, :, pl.ds(i * 128, 128)], zp))
    at = lanes(zh * HALF2, HALF2)
    mine = (dot(w2t[...], taps2[:, at]) + bias).astype(BF)
    spat[:, at] = mine
    raw2[1, zh] = mine
    y2_own = to_frames(raw2, zh, 0, HALF2)
    wide = spat[...].astype(F32)
    q2_iota = lax.broadcasted_iota(jnp.int32, (Q2, 1), 0)
    row3 = group_row(
        jnp.sum(wide, axis=1, keepdims=True),
        jnp.sum(wide * wide, axis=1, keepdims=True),
        q2_iota + c * Q2,
        C2 // GROUPS,
    )
    state = stat_send(row3, x_peers)
    y2_fwd = []

    def forward2(i):
        z2[i].wait_recv()
        y2_fwd.append(to_frames(raw2, oz, i * 128, 128))

    state = stat_send(stat_wait(state), y_peers)
    forward2(0)
    state = stat_send(stat_wait(state), chan_peers)
    forward2(1)
    forward2(2)
    total = stat_wait(state)
    affine3 = [
        scale_columns(
            total,
            float(C2 // GROUPS * POS2 * frames),
            q2_iota + (2 * z + k) * Q2,
            C2 // GROUPS,
            cols[z][0:Q2, 2:3],
            cols[z][0:Q2, 3:4],
        )
        for z in range(2)
    ]
    hid2 = r["hid2"]
    k2 = []
    for i in range(TILES):
        k2.append([hidden(raw2, hid2, zh, affine3, i * 128, 128, y2_own if i == 0 else [Done()] * 2)])
        k2[i].append(hidden(raw2, hid2, oz, affine3, i * 128, 128, y2_fwd[i]))

    fin, fin_rx = r["fin"], r["fin_rx"]

    def second_conv(z, at, n):
        mixed = sum(
            dot(w4t[slot, z], hid2[slot, :, :, :, at].reshape(6 * Q2, n)) for slot in range(2)
        ).astype(BF)
        return (raw2[1, z, :, at].astype(F32) + mixed.astype(F32)).astype(BF)

    last = []
    for i in range(TILES):
        for copy in k2[i]:
            copy.wait_recv()
        at = slice(i * 128, (i + 1) * 128)
        fin[:, at] = second_conv(oz, at, 128)
        last.append(send(fin.at[:, pl.ds(i * 128, 128)], fin_rx.at[:, pl.ds(i * 128, 128)], zp))
    out[:, lanes(zh * HALF2, HALF2)] = second_conv(zh, slice(0, HALF2), HALF2)
    for copy in last:
        copy.wait_recv()
    out[:, lanes(oz * HALF2, HALF2)] = fin_rx[...]
    for copy in sent:
        copy.wait_send()


def per_device(frames, lat, tw1, g1, s1, dw, g2, s2, cw2, sw2, tb, tw2, g3, s3):
    vmem = pl.BlockSpec(memory_space=pltpu.VMEM)
    far = pl.BlockSpec(memory_space=pl.ANY)
    row = lambda v: v.reshape(1, v.shape[0])
    result = pl.pallas_call(
        functools.partial(kernel, frames),
        out_shape=jax.ShapeDtypeStruct((Q2, POS2), BF),
        in_specs=[far, far, vmem, vmem, far, vmem, vmem, far, far, vmem, far, vmem, vmem],
        out_specs=vmem,
        scratch_shapes=[pltpu.VMEM(shape, dtype) for shape, dtype in SCRATCH.values()]
        + [
            pltpu.SemaphoreType.DMA((N_SEM,)),
            pltpu.SemaphoreType.DMA((N_SEM,)),
            pltpu.SemaphoreType.DMA((8,)),
        ],
        compiler_params=pltpu.CompilerParams(
            collective_id=0, has_side_effects=True, vmem_limit_bytes=56 * 2**20
        ),
        name="video_block",
    )(
        lat.reshape(Q1, H1 * W1),
        tw1.reshape(3 * C1, C1),
        row(g1),
        row(s1),
        dw.reshape(9 * Q1, C1),
        g2,
        s2,
        cw2.transpose(0, 2, 1).reshape(9 * Q2, C1),
        sw2.T,
        row(tb),
        tw2.reshape(3 * C2, C2),
        row(g3),
        row(s3),
    )
    return result.reshape(1, Q2, POS2)


def solution(mesh):
    return jax.shard_map(
        functools.partial(per_device, mesh.shape["frame"]),
        mesh=mesh,
        in_specs=(
            P(("video", "frame"), "chan", None),
            P(),
            P("chan"),
            P("chan"),
            P(None, "chan", None),
            P(),
            P(),
            P(None, None, "chan"),
            P(None, "chan"),
            P("chan"),
            P(),
            P("chan"),
            P("chan"),
        ),
        out_specs=P(("video", "frame"), "chan", None),
        check_vma=False,
    )
```

time: 97.8 us -> 80.8 us (0.83)
  the two profiles are of different devices: /device:TPU:65 before, /device:TPU:129 now
where the time goes in v2:
time: 80.8 us; the launch traced here: 80.7 us
  Pallas kernels  79 us (98%)
  local copies, waits for them, and re-layouts  1.65 us (2%)
    pallas_call x1, Pallas kernels, per_device(): pl.pallas_call(functools.partial(kernel, frames), out_shape=jax.ShapeDtyp...  79 us
    unnamed x1, local copies, waits for them, and re-layouts  1.65 us

profile of v2, /device:TPU:129, one launch (start us, length us, event | category | flops | bytes accessed | tf_op | source)
XLA Modules:
  0.0 80.7 jit_solution(16799673074486712102)
XLA Ops:
  0.0 79.0 %video_block.1 = bf16[160,768]{1,0:T(8,128)(2,1)} custom-call(bf16[80,3072]{1,0:T(8,128)(2,1)} %bitcast.19, bf16[960,320]{1,0:T(8,128)(2,1)} %bitcast.17, f32[1,80]{1,0:T(1,128)} %bitcast.24, f32[1,80]{1,0:T(1,128)} %bitcast.25, bf16[720,320]{1,0:T(8,128)(2,1)} %bitcast.18, f32[320]{0:T(512)} %refs_5_.1, f32[320]{0:T(512)} %refs_6_.1, ...), custom_call_target="tpu_custom_call" | custom-call | tf_op jit(solution)/shard_map/video_block/pallas_call | solution.py:548
  79.0 1.7 %copy.15 = bf16[1,160,768]{2,1,0:T(8,128)(2,1)} copy(bf16[1,160,768]{2,1,0:T(8,128)(2,1)} %bitcast.16) | data formatting | bytes 491520

commit v3 on v2

--- a/solution.py
+++ b/solution.py
@@ -49,19 +49,26 @@
     "part_rx": ((C1 // 2, HALF2), F32),
     "red": ((2, 2, C1 // 2, HALF2), BF),
     "nrm": ((C1, POS2 + 256), BF),
-    "taps2": ((10 * C1, POS2), BF),
+    "taps2": ((10 * C1, HALF2), BF),
+    "taps2o": ((10 * C1, HALF2), BF),
     "w2t": ((Q2, 10 * C1), BF),
-    "spat": ((Q2, POS2), BF),
-    "raw2": ((3, 2, Q2, HALF2), BF),
+    "spat_o": ((Q2, HALF2), BF),
+    "raw2": ((2, 3, 2, Q2, HALF2), BF),
     "hid2": ((2, 3, 2, Q2, HALF2), BF),
     "tmp2": ((C2, 6 * Q2), BF),
     "w4t": ((2, 2, Q2, 6 * Q2), BF),
     "pick1": ((256, 384), BF),
     "pick2": ((3, 256, 256), BF),
-    "fin": ((Q2, HALF2), BF),
-    "fin_rx": ((Q2, HALF2), BF),
-    "par": ((2, 8, 256), F32),
+    "fin": ((2, Q2, HALF2), BF),
+    "par": ((2, 2, 8, 256), F32),
     "par2": ((8, 384), F32),
+    "g1_v": ((1, Q1), F32),
+    "s1_v": ((1, Q1), F32),
+    "g2_v": ((C1,), F32),
+    "s2_v": ((C1,), F32),
+    "g3_v": ((1, Q2), F32),
+    "s3_v": ((1, Q2), F32),
+    "tb_v": ((1, Q2), F32),
     "st_tx": ((6, 1, 128), F32),
     "st_rx": ((32, 1, 128), F32),
 }
@@ -100,11 +107,6 @@
     square = jnp.sum(jnp.where(second, row, 0.0), axis=1, keepdims=True) / count
     scale = lax.rsqrt(square - mean * mean + EPS) * gain
     return 0.5 * scale, 0.5 * (shift - mean * scale)
-
-
-class Done:
-    def wait_recv(self):
-        pass
 
 
 def kernel(frames, *refs):
@@ -126,11 +128,23 @@
     x_peers = [{"frame": lax.rem(x + d, NX) * ny + y} for d in range(1, NX)]
     y_peers = [{"frame": x * ny + lax.rem(y + d, ny)} for d in range(1, ny)]
 
+    barrier = pltpu.get_barrier_semaphore()
+    greeted = chan_peers + x_peers + y_peers + [after, before]
+    for peer in greeted:
+        pl.semaphore_signal(barrier, inc=1, device_id=peer, device_id_type=MESH)
+
     loads = {}
     for number, (name, ref, dst) in enumerate(
         (
             ("lat", lat, r["lat_v"]),
             ("dw", dw, r["dwt"].at[zh, pl.ds(0, 9 * Q1)]),
+            ("g1", g1, r["g1_v"]),
+            ("s1", s1, r["s1_v"]),
+            ("g2", g2, r["g2_v"]),
+            ("s2", s2, r["s2_v"]),
+            ("g3", g3, r["g3_v"]),
+            ("s3", s3, r["s3_v"]),
+            ("tb", tb, r["tb_v"]),
             ("tw1", tw1, r["tw1_v"]),
             ("cw2", cw2, r["cw2_v"]),
             ("sw2", sw2, r["sw2_v"]),
@@ -139,11 +153,6 @@
     ):
         loads[name] = pltpu.make_async_copy(ref, dst, local_sem.at[number])
         loads[name].start()
-
-    barrier = pltpu.get_barrier_semaphore()
-    greeted = chan_peers + x_peers + y_peers + [after, before]
-    for peer in greeted:
-        pl.semaphore_signal(barrier, inc=1, device_id=peer, device_id_type=MESH)
 
     counter = [0]
     sent = []
@@ -188,13 +197,6 @@
     lat_v = r["lat_v"]
 
     par = r["par"]
-    par[zh, 0:1, 0:Q1] = g1[...]
-    par[zh, 1:2, 0:Q1] = s1[...]
-    par[zh, 2:3, 0:Q2] = g3[...]
-    par[zh, 3:4, 0:Q2] = s3[...]
-    par[zh, 4:5, 0:Q2] = tb[...]
-    r["par2"][0:1, 0:C1] = g2[...].reshape(1, C1)
-    r["par2"][1:2, 0:C1] = s2[...].reshape(1, C1)
     loads["lat"].wait()
     zsrc = r["zsrc"]
     raw1[1, zh, :, 0:W1] = lat_v[:, HALF1 - W1 : HALF1]
@@ -210,7 +212,15 @@
         C1 // GROUPS,
     )
     dwt = r["dwt"]
-    loads["dw"].wait()
+    for name in ("dw", "g1", "s1", "g2", "s2", "g3", "s3", "tb"):
+        loads[name].wait()
+    par[0, zh, 0:1, 0:Q1] = r["g1_v"][...]
+    par[0, zh, 1:2, 0:Q1] = r["s1_v"][...]
+    par[0, zh, 2:3, 0:Q2] = r["g3_v"][...]
+    par[0, zh, 3:4, 0:Q2] = r["s3_v"][...]
+    par[0, zh, 4:5, 0:Q2] = r["tb_v"][...]
+    r["par2"][0:1, 0:C1] = r["g2_v"][...].reshape(1, C1)
+    r["par2"][1:2, 0:C1] = r["s2_v"][...].reshape(1, C1)
     dwt[zh, 9 * Q1 : DPAD, :] = jnp.zeros((DPAD - 9 * Q1, C1), BF)
     pl.semaphore_wait(barrier, len(greeted))
 
@@ -218,7 +228,6 @@
     pieces = ny // 2
     piece = DPART // pieces
     own_piece = pl.ds(pl.multiple_of(x * DPART + (y // 2) * piece, 16), piece)
-    own_part = pl.ds(pl.multiple_of(x * DPART, 16), DPART)
     dw_z = send(dwt.at[zh, own_piece], dwt.at[zh, own_piece], zp)
 
     z_copies = [
@@ -233,7 +242,7 @@
         ]
 
     y_own = [to_frames(raw1, zh, a, n) for a, n in CHUNKS]
-    par_copy = send(par.at[zh], par.at[zh], zp)
+    par_copy = send(par.at[0, zh], par.at[0, zh], zp)
 
     def prepare(weight, held, store, width, count, slot, core):
         rows = [
@@ -273,6 +282,7 @@
     dw_y = [
         send(here, here, {"frame": x * ny + lax.rem(y + 2 * d, ny)}) for d in range(1, pieces)
     ]
+    dw_x = [send(here, here, p) for p in x_peers]
 
     src = lax.broadcasted_iota(jnp.int32, (256, 256), 0)
     dst = lax.broadcasted_iota(jnp.int32, (256, 256), 1)
@@ -290,7 +300,6 @@
     for t in range(9):
         w2t[:, t * C1 : (t + 1) * C1] = r["cw2_v"][t * Q2 : (t + 1) * Q2, :]
     w2t[:, 9 * C1 : 10 * C1] = r["sw2_v"][...]
-    state = stat_send(stat_wait(state), y_peers)
     y_fwd = []
 
     def forward(i):
@@ -298,11 +307,19 @@
         y_fwd.append(to_frames(raw1, oz, *CHUNKS[i]))
 
     forward(0)
+    state = stat_send(stat_wait(state), y_peers)
+    for d in range(1, pieces):
+        dw_y[d - 1].wait_recv()
+        start = x * DPART + lax.rem(y // 2 + pieces - d, pieces) * piece
+        there = dwt.at[oz, pl.ds(pl.multiple_of(start, 16), piece)]
+        dw_x += [send(there, there, p) for p in x_peers]
+    forward(1)
     loads["tw2"].wait()
     for slot, core in ((0, k), (1, ok)):
         prepare(r["tw2_v"], r["tmp2"], store4, C2, Q2, slot, core)
     par_copy.wait_recv()
-    cols = [to_columns(par[z]) for z in range(2)]
+    par_k = send(par.at[0], par.at[1], kp)
+    cols = [to_columns(par[0, z]) for z in range(2)]
     cols2 = to_columns(r["par2"][...])
     bias = jnp.where(zh == 0, cols[0][0:Q2, 4:5], cols[1][0:Q2, 4:5])
     total = stat_wait(state)
@@ -317,11 +334,6 @@
         )
         for z in range(2)
     ]
-    for copy in dw_y:
-        copy.wait_recv()
-    other_part = dwt.at[oz, own_part]
-    dw_x = [send(other_part, other_part, p) for p in x_peers]
-    forward(1)
     hid1 = r["hid1"]
     alive = {0: f > 0, 2: f < frames - 1}
 
@@ -413,11 +425,11 @@
     hid_own(0)
     hid_other(0)
     hid_own(1)
+    forward(2)
+    first_conv(0)
     hid_other(1)
-    first_conv(0)
-    forward(2)
+    hid_own(2)
     first_conv(1)
-    hid_own(2)
     for copy in dw_x:
         copy.wait_recv()
     down(0)
@@ -434,7 +446,7 @@
         for copy in red_k[i]:
             copy.wait_recv()
 
-    nrm, taps2 = r["nrm"], r["taps2"]
+    nrm = r["nrm"]
     nrm[:, 0:128] = jnp.zeros((C1, 128), BF)
     nrm[:, 128 + POS2 :] = jnp.zeros((C1, 128), BF)
     half_iota = lax.broadcasted_iota(jnp.int32, (half, 1), 0)
@@ -453,34 +465,36 @@
             row2, float(C1 // GROUPS * POS2), chan, C1 // GROUPS, cols2[span, 0:1], cols2[span, 1:2]
         )
         nrm[span, 128 : 128 + POS2] = silu_of_half(wide * scale + shift).astype(BF)
-        for z in range(2):
-            taps2[9 * C1 + core * half : 9 * C1 + (core + 1) * half, z * HALF2 : (z + 1) * HALF2] = (
-                sides[z]
-            )
-
-    for dx in range(3):
-        for j in range(POS2 // 128 + 1):
-            got = dot(nrm[:, j * 128 : j * 128 + 256], r["pick2"][dx]).astype(BF)
-            if j < POS2 // 128:
-                at = slice(j * 128, (j + 1) * 128)
-                taps2[dx * C1 : (dx + 1) * C1, at] = got[:, 0:128]
-                taps2[(3 + dx) * C1 : (4 + dx) * C1, at] = got[:, 128:256]
-            if j > 0:
-                at = slice((j - 1) * 128, j * 128)
-                taps2[(6 + dx) * C1 : (7 + dx) * C1, at] = got[:, 0:128]
-
-    spat = r["spat"]
+
+    def second(side, taps):
+        for dx in range(3):
+            for j in range(TILES + 1):
+                window = nrm[:, lanes(side * HALF2 + j * 128, 256)]
+                got = dot(window, r["pick2"][dx]).astype(BF)
+                if j < TILES:
+                    at = slice(j * 128, (j + 1) * 128)
+                    taps[dx * C1 : (dx + 1) * C1, at] = got[:, 0:128]
+                    taps[(3 + dx) * C1 : (4 + dx) * C1, at] = got[:, 128:256]
+                if j > 0:
+                    at = slice((j - 1) * 128, j * 128)
+                    taps[(6 + dx) * C1 : (7 + dx) * C1, at] = got[:, 0:128]
+        for core in range(2):
+            taps[9 * C1 + core * half : 9 * C1 + (core + 1) * half, :] = red[core, side]
+
+    spat_o = r["spat_o"]
+    second(oz, r["taps2o"])
     z2 = []
     for i in range(TILES):
-        at = lanes(oz * HALF2 + i * 128, 128)
-        spat[:, at] = (dot(w2t[...], taps2[:, at]) + bias).astype(BF)
-        z2.append(send(spat.at[:, at], raw2.at[1, zh, :, pl.ds(i * 128, 128)], zp))
-    at = lanes(zh * HALF2, HALF2)
-    mine = (dot(w2t[...], taps2[:, at]) + bias).astype(BF)
-    spat[:, at] = mine
-    raw2[1, zh] = mine
-    y2_own = to_frames(raw2, zh, 0, HALF2)
-    wide = spat[...].astype(F32)
+        at = slice(i * 128, (i + 1) * 128)
+        spat_o[:, at] = (dot(w2t[...], r["taps2o"][:, at]) + bias).astype(BF)
+        here = pl.ds(i * 128, 128)
+        z2.append(send(spat_o.at[:, here], raw2.at[0, 1, zh, :, here], zp))
+    second(zh, r["taps2"])
+    raw2[0, 1, zh] = (dot(w2t[...], r["taps2"][...]) + bias).astype(BF)
+    own = raw2.at[0]
+    y2_own = to_frames(own, zh, 0, HALF2)
+    raw_k = [send(raw2.at[0, 1, zh], raw2.at[1, 1, zh], kp)]
+    wide = jnp.concatenate([raw2[0, 1, zh], spat_o[...]], axis=1).astype(F32)
     q2_iota = lax.broadcasted_iota(jnp.int32, (Q2, 1), 0)
     row3 = group_row(
         jnp.sum(wide, axis=1, keepdims=True),
@@ -489,72 +503,89 @@
         C2 // GROUPS,
     )
     state = stat_send(row3, x_peers)
+    par_k.wait_recv()
+    cols3 = [cols, [to_columns(par[1, z]) for z in range(2)]]
     y2_fwd = []
+
+    def share(tap, z, a, n):
+        here = pl.ds(a, n)
+        raw_k.append(send(raw2.at[0, tap, z, :, here], raw2.at[1, tap, z, :, here], kp))
 
     def forward2(i):
         z2[i].wait_recv()
-        y2_fwd.append(to_frames(raw2, oz, i * 128, 128))
+        y2_fwd.append(to_frames(own, oz, i * 128, 128))
+        share(1, oz, i * 128, 128)
 
     state = stat_send(stat_wait(state), y_peers)
+    for tap in (0, 2):
+        y2_own[tap // 2].wait_recv()
+        share(tap, zh, 0, HALF2)
     forward2(0)
     state = stat_send(stat_wait(state), chan_peers)
     forward2(1)
     forward2(2)
+    for i in range(TILES):
+        for tap in (0, 2):
+            y2_fwd[i][tap // 2].wait_recv()
+            share(tap, oz, i * 128, 128)
     total = stat_wait(state)
-    affine3 = [
-        scale_columns(
-            total,
-            float(C2 // GROUPS * POS2 * frames),
-            q2_iota + (2 * z + k) * Q2,
-            C2 // GROUPS,
-            cols[z][0:Q2, 2:3],
-            cols[z][0:Q2, 3:4],
-        )
-        for z in range(2)
-    ]
     hid2 = r["hid2"]
-    k2 = []
-    for i in range(TILES):
-        k2.append([hidden(raw2, hid2, zh, affine3, i * 128, 128, y2_own if i == 0 else [Done()] * 2)])
-        k2[i].append(hidden(raw2, hid2, oz, affine3, i * 128, 128, y2_fwd[i]))
-
-    fin, fin_rx = r["fin"], r["fin_rx"]
+    for slot, core in ((0, k), (1, ok)):
+        if slot == 1:
+            for copy in raw_k:
+                copy.wait_recv()
+        for z in range(2):
+            scale, shift = scale_columns(
+                total,
+                float(C2 // GROUPS * POS2 * frames),
+                q2_iota + (2 * z + core) * Q2,
+                C2 // GROUPS,
+                cols3[slot][z][0:Q2, 2:3],
+                cols3[slot][z][0:Q2, 3:4],
+            )
+            for tap in range(3):
+                value = silu_of_half(raw2[slot, tap, z].astype(F32) * scale + shift)
+                if tap != 1:
+                    value = jnp.where(alive[tap], value, 0.0)
+                hid2[slot, tap, z] = value.astype(BF)
+
+    fin = r["fin"]
 
     def second_conv(z, at, n):
         mixed = sum(
             dot(w4t[slot, z], hid2[slot, :, :, :, at].reshape(6 * Q2, n)) for slot in range(2)
         ).astype(BF)
-        return (raw2[1, z, :, at].astype(F32) + mixed.astype(F32)).astype(BF)
+        return (raw2[0, 1, z, :, at].astype(F32) + mixed.astype(F32)).astype(BF)
 
     last = []
     for i in range(TILES):
-        for copy in k2[i]:
-            copy.wait_recv()
         at = slice(i * 128, (i + 1) * 128)
-        fin[:, at] = second_conv(oz, at, 128)
-        last.append(send(fin.at[:, pl.ds(i * 128, 128)], fin_rx.at[:, pl.ds(i * 128, 128)], zp))
-    out[:, lanes(zh * HALF2, HALF2)] = second_conv(zh, slice(0, HALF2), HALF2)
+        fin[0, :, at] = second_conv(oz, at, 128)
+        there = out.at[:, lanes(zh * HALF2 + i * 128, 128)]
+        last.append(send(fin.at[0, :, pl.ds(i * 128, 128)], there, zp))
+    fin[1] = second_conv(zh, slice(0, HALF2), HALF2)
+    kept = pltpu.make_async_copy(fin.at[1], out.at[:, lanes(zh * HALF2, HALF2)], local_sem.at[15])
+    kept.start()
     for copy in last:
         copy.wait_recv()
-    out[:, lanes(oz * HALF2, HALF2)] = fin_rx[...]
+    kept.wait()
     for copy in sent:
         copy.wait_send()
 
 
 def per_device(frames, lat, tw1, g1, s1, dw, g2, s2, cw2, sw2, tb, tw2, g3, s3):
-    vmem = pl.BlockSpec(memory_space=pltpu.VMEM)
     far = pl.BlockSpec(memory_space=pl.ANY)
     row = lambda v: v.reshape(1, v.shape[0])
     result = pl.pallas_call(
         functools.partial(kernel, frames),
         out_shape=jax.ShapeDtypeStruct((Q2, POS2), BF),
-        in_specs=[far, far, vmem, vmem, far, vmem, vmem, far, far, vmem, far, vmem, vmem],
-        out_specs=vmem,
+        in_specs=[far] * 13,
+        out_specs=far,
         scratch_shapes=[pltpu.VMEM(shape, dtype) for shape, dtype in SCRATCH.values()]
         + [
             pltpu.SemaphoreType.DMA((N_SEM,)),
             pltpu.SemaphoreType.DMA((N_SEM,)),
-            pltpu.SemaphoreType.DMA((8,)),
+            pltpu.SemaphoreType.DMA((16,)),
         ],
         compiler_params=pltpu.CompilerParams(
             collective_id=0, has_side_effects=True, vmem_limit_bytes=56 * 2**20

time: 80.8 us -> 78.7 us (0.974)
  Pallas kernels: 79 us -> 76.9 us
    pallas_call x1, Pallas kernels: 79 us -> 76.9 us  [per_device(): pl.pallas_call(functools.partial(kernel, frames), out_shape=jax.ShapeDtyp...]
where the time goes in v3:
time: 78.7 us; the launch traced here: 78.6 us
  Pallas kernels  76.9 us (98%)
  local copies, waits for them, and re-layouts  1.65 us (2%)
    pallas_call x1, Pallas kernels, per_device(): pl.pallas_call(functools.partial(kernel, frames), out_shape=jax.ShapeDtyp...  76.9 us
    unnamed x1, local copies, waits for them, and re-layouts  1.65 us

profile of v3, /device:TPU:129, one launch (start us, length us, event | category | flops | bytes accessed | tf_op | source)
XLA Modules:
  0.0 78.6 jit_solution(13297379047329003841)
XLA Ops:
  0.0 76.9 %video_block.1 = bf16[160,768]{1,0:T(8,128)(2,1)} custom-call(bf16[80,3072]{1,0:T(8,128)(2,1)} %bitcast.19, bf16[960,320]{1,0:T(8,128)(2,1)} %bitcast.17, f32[1,80]{1,0:T(1,128)} %bitcast.24, f32[1,80]{1,0:T(1,128)} %bitcast.25, bf16[720,320]{1,0:T(8,128)(2,1)} %bitcast.18, f32[320]{0:T(512)} %refs_5_.1, f32[320]{0:T(512)} %refs_6_.1, ...), custom_call_target="tpu_custom_call" | custom-call | tf_op jit(solution)/shard_map/video_block/pallas_call | solution.py:579
  76.9 1.7 %copy.15 = bf16[1,160,768]{2,1,0:T(8,128)(2,1)} copy(bf16[1,160,768]{2,1,0:T(8,128)(2,1)} %bitcast.16) | data formatting | bytes 491520

commit v4 on v3

--- a/solution.py
+++ b/solution.py
@@ -29,6 +29,9 @@
 DPAD = 768
 DPART = DPAD // NX
 TILES = HALF2 // 128
+KTILES = 10 * C1 // 128
+CROWS = 4096
+CPART = CROWS // NX
 CHUNKS = ((0, 640), (640, 512), (1152, 512))
 
 SCRATCH = {
@@ -47,12 +50,12 @@
     "taps1": ((2, 9 * Q1, HALF2), BF),
     "part": ((C1, HALF2), F32),
     "part_rx": ((C1 // 2, HALF2), F32),
-    "red": ((2, 2, C1 // 2, HALF2), BF),
-    "nrm": ((C1, POS2 + 256), BF),
+    "red": ((2, C1 // 2, HALF2), BF),
+    "halo": ((2, C1 // 2, 128), BF),
+    "nrm": ((C1, HALF2 + 256), BF),
     "taps2": ((10 * C1, HALF2), BF),
-    "taps2o": ((10 * C1, HALF2), BF),
     "w2t": ((Q2, 10 * C1), BF),
-    "spat_o": ((Q2, HALF2), BF),
+    "cwt": ((2, CROWS, 128), BF),
     "raw2": ((2, 3, 2, Q2, HALF2), BF),
     "hid2": ((2, 3, 2, Q2, HALF2), BF),
     "tmp2": ((C2, 6 * Q2), BF),
@@ -69,8 +72,8 @@
     "g3_v": ((1, Q2), F32),
     "s3_v": ((1, Q2), F32),
     "tb_v": ((1, Q2), F32),
-    "st_tx": ((6, 1, 128), F32),
-    "st_rx": ((32, 1, 128), F32),
+    "st_tx": ((8, 1, 128), F32),
+    "st_rx": ((40, 1, 128), F32),
 }
 N_SEM = 128
 
@@ -128,8 +131,16 @@
     x_peers = [{"frame": lax.rem(x + d, NX) * ny + y} for d in range(1, NX)]
     y_peers = [{"frame": x * ny + lax.rem(y + d, ny)} for d in range(1, ny)]
 
+    xz_peers = [
+        {"frame": lax.rem(x + d, NX) * ny + y, "chan": lax.rem(c + e, 4)}
+        for d in range(NX)
+        for e in (0, 2)
+        if d or e
+    ]
+    diagonal = {"chan": lax.rem(c + 2, 4) + 1 - 2 * k}
+
     barrier = pltpu.get_barrier_semaphore()
-    greeted = chan_peers + x_peers + y_peers + [after, before]
+    greeted = xz_peers + y_peers + [kp, diagonal, after, before]
     for peer in greeted:
         pl.semaphore_signal(barrier, inc=1, device_id=peer, device_id_type=MESH)
 
@@ -224,7 +235,7 @@
     dwt[zh, 9 * Q1 : DPAD, :] = jnp.zeros((DPAD - 9 * Q1, C1), BF)
     pl.semaphore_wait(barrier, len(greeted))
 
-    state = stat_send(row1, chan_peers)
+    state = stat_send(row1, xz_peers)
     pieces = ny // 2
     piece = DPART // pieces
     own_piece = pl.ds(pl.multiple_of(x * DPART + (y // 2) * piece, 16), piece)
@@ -276,7 +287,22 @@
             same & (src_col == 2 * dst_col + dx - 1), 1.0, 0.0
         ).astype(BF)
 
-    state = stat_send(stat_wait(state), x_peers)
+    loads["cw2"].wait()
+    loads["sw2"].wait()
+    cwt = r["cwt"]
+    for t in range(9):
+        w2t[:, t * C1 : (t + 1) * C1] = r["cw2_v"][t * Q2 : (t + 1) * Q2, :]
+    w2t[:, 9 * C1 : 10 * C1] = r["sw2_v"][...]
+    for j in range(KTILES):
+        cwt[zh, j * Q2 : (j + 1) * Q2, :] = w2t[:, j * 128 : (j + 1) * 128]
+    cwt[zh, KTILES * Q2 :, :] = jnp.zeros((CROWS - KTILES * Q2, 128), BF)
+    cpiece = CPART // pieces
+
+    def cw_rows(d):
+        start = x * CPART + lax.rem(y // 2 + pieces - d, pieces) * cpiece
+        return pl.ds(pl.multiple_of(start, 16), cpiece)
+
+    cw_z = send(cwt.at[zh, cw_rows(0)], cwt.at[zh, cw_rows(0)], zp)
     dw_z.wait_recv()
     here = dwt.at[oz, own_piece]
     dw_y = [
@@ -295,11 +321,6 @@
         want = col + (dx - 1)
         keep = (want >= 0) & (want < W2) & (src == base + want)
         r["pick2"][dx] = jnp.where(keep, 1.0, 0.0).astype(BF)
-    loads["cw2"].wait()
-    loads["sw2"].wait()
-    for t in range(9):
-        w2t[:, t * C1 : (t + 1) * C1] = r["cw2_v"][t * Q2 : (t + 1) * Q2, :]
-    w2t[:, 9 * C1 : 10 * C1] = r["sw2_v"][...]
     y_fwd = []
 
     def forward(i):
@@ -319,9 +340,9 @@
         prepare(r["tw2_v"], r["tmp2"], store4, C2, Q2, slot, core)
     par_copy.wait_recv()
     par_k = send(par.at[0], par.at[1], kp)
+    state = stat_send(stat_wait(state), [kp])
     cols = [to_columns(par[0, z]) for z in range(2)]
     cols2 = to_columns(r["par2"][...])
-    bias = jnp.where(zh == 0, cols[0][0:Q2, 4:5], cols[1][0:Q2, 4:5])
     total = stat_wait(state)
     affine1 = [
         scale_columns(
@@ -355,7 +376,7 @@
     blk, taps1 = r["blk"], r["taps1"]
     part, part_rx, red = r["part"], r["part_rx"], r["red"]
     half = C1 // 2
-    k1, part_k, red_z, red_k = {}, {}, {}, {}
+    k1, part_k, red_k = {}, {}, {}
 
     def hid_own(i):
         k1[i] = [hidden(raw1, hid1, zh, affine1, *CHUNKS[i], y_own[i])]
@@ -412,20 +433,20 @@
         at = slice(i * 128, (i + 1) * 128)
         part_k[i].wait_recv()
         mine = part[pl.ds(pl.multiple_of(k * half, 16), half), at]
-        red[k, zh, :, at] = (mine + part_rx[:, at]).astype(BF)
-        here = red.at[k, zh, :, pl.ds(i * 128, 128)]
-        red_z[i] = send(here, here, zp)
-        red_k[i] = [send(here, here, kp)]
-
-    def pass_reduced(i):
-        red_z[i].wait_recv()
-        here = red.at[k, oz, :, pl.ds(i * 128, 128)]
-        red_k[i].append(send(here, here, kp))
+        red[k, :, at] = (mine + part_rx[:, at]).astype(BF)
+        here = red.at[k, :, pl.ds(i * 128, 128)]
+        red_k[i] = send(here, here, kp)
 
     hid_own(0)
     hid_other(0)
     hid_own(1)
     forward(2)
+    cw_z.wait_recv()
+    here = cwt.at[oz, cw_rows(0)]
+    cw_y = [
+        send(here, here, {"frame": x * ny + lax.rem(y + 2 * d, ny)}) for d in range(1, pieces)
+    ]
+    cw_x = [send(here, here, p) for p in x_peers]
     first_conv(0)
     hid_other(1)
     hid_own(2)
@@ -440,94 +461,85 @@
     first_conv(2)
     down(2)
     reduced(2)
-    for i in range(3):
-        pass_reduced(i)
-    for i in range(3):
-        for copy in red_k[i]:
-            copy.wait_recv()
-
-    nrm = r["nrm"]
-    nrm[:, 0:128] = jnp.zeros((C1, 128), BF)
-    nrm[:, 128 + POS2 :] = jnp.zeros((C1, 128), BF)
+
     half_iota = lax.broadcasted_iota(jnp.int32, (half, 1), 0)
+    wide = red[k].astype(F32)
+    row2 = group_row(
+        jnp.sum(wide, axis=1, keepdims=True),
+        jnp.sum(wide * wide, axis=1, keepdims=True),
+        half_iota + k * half,
+        C1 // GROUPS,
+    )
+    state = stat_send(row2, chan_peers)
+    edge = red.at[k, :, lanes(oz * (HALF2 - 128), 128)]
+    halo = r["halo"]
+    edges = [send(edge, halo.at[k], p) for p in (zp, diagonal)]
+    for d in range(1, pieces):
+        cw_y[d - 1].wait_recv()
+        there = cwt.at[oz, cw_rows(d)]
+        cw_x += [send(there, there, p) for p in x_peers]
+    for i in range(TILES):
+        red_k[i].wait_recv()
+    total2 = stat_wait(state)
+    for copy in edges:
+        copy.wait_recv()
+    nrm, taps2 = r["nrm"], r["taps2"]
     for core in range(2):
-        sides = [red[core, z] for z in range(2)]
-        wide = jnp.concatenate(sides, axis=1).astype(F32)
-        chan = half_iota + core * half
-        row2 = group_row(
+        span = slice(core * half, (core + 1) * half)
+        scale, shift = scale_columns(
+            total2,
+            float(C1 // GROUPS * POS2),
+            half_iota + core * half,
+            C1 // GROUPS,
+            cols2[span, 0:1],
+            cols2[span, 1:2],
+        )
+        nrm[span, 128 : 128 + HALF2] = silu_of_half(red[core].astype(F32) * scale + shift).astype(BF)
+        outer = silu_of_half(halo[core].astype(F32) * scale + shift)
+        nrm[span, 0:128] = jnp.where(zh == 1, outer, 0.0).astype(BF)
+        nrm[span, 128 + HALF2 :] = jnp.where(zh == 0, outer, 0.0).astype(BF)
+        taps2[9 * C1 + core * half : 9 * C1 + (core + 1) * half, :] = red[core]
+
+    for dx in range(3):
+        for j in range(TILES + 1):
+            got = dot(nrm[:, j * 128 : j * 128 + 256], r["pick2"][dx]).astype(BF)
+            if j < TILES:
+                at = slice(j * 128, (j + 1) * 128)
+                taps2[dx * C1 : (dx + 1) * C1, at] = got[:, 0:128]
+                taps2[(3 + dx) * C1 : (4 + dx) * C1, at] = got[:, 128:256]
+            if j > 0:
+                at = slice((j - 1) * 128, j * 128)
+                taps2[(6 + dx) * C1 : (7 + dx) * C1, at] = got[:, 0:128]
+    for copy in cw_x:
+        copy.wait_recv()
+    own = raw2.at[0]
+    y2 = []
+    for z in range(2):
+        weight = jnp.concatenate(
+            [cwt[z, j * Q2 : (j + 1) * Q2, :] for j in range(KTILES)], axis=1
+        )
+        raw2[0, 1, z] = (dot(weight, taps2[...]) + cols[z][0:Q2, 4:5]).astype(BF)
+        y2.append(to_frames(own, z, 0, HALF2))
+    raw_k = [send(raw2.at[0, 1], raw2.at[1, 1], kp)]
+    q2_iota = lax.broadcasted_iota(jnp.int32, (Q2, 1), 0)
+    row3 = jnp.zeros((1, 128), F32)
+    for z in range(2):
+        wide = raw2[0, 1, z].astype(F32)
+        row3 = row3 + group_row(
             jnp.sum(wide, axis=1, keepdims=True),
             jnp.sum(wide * wide, axis=1, keepdims=True),
-            chan,
-            C1 // GROUPS,
-        )
-        span = slice(core * half, (core + 1) * half)
-        scale, shift = scale_columns(
-            row2, float(C1 // GROUPS * POS2), chan, C1 // GROUPS, cols2[span, 0:1], cols2[span, 1:2]
-        )
-        nrm[span, 128 : 128 + POS2] = silu_of_half(wide * scale + shift).astype(BF)
-
-    def second(side, taps):
-        for dx in range(3):
-            for j in range(TILES + 1):
-                window = nrm[:, lanes(side * HALF2 + j * 128, 256)]
-                got = dot(window, r["pick2"][dx]).astype(BF)
-                if j < TILES:
-                    at = slice(j * 128, (j + 1) * 128)
-                    taps[dx * C1 : (dx + 1) * C1, at] = got[:, 0:128]
-                    taps[(3 + dx) * C1 : (4 + dx) * C1, at] = got[:, 128:256]
-                if j > 0:
-                    at = slice((j - 1) * 128, j * 128)
-                    taps[(6 + dx) * C1 : (7 + dx) * C1, at] = got[:, 0:128]
-        for core in range(2):
-            taps[9 * C1 + core * half : 9 * C1 + (core + 1) * half, :] = red[core, side]
-
-    spat_o = r["spat_o"]
-    second(oz, r["taps2o"])
-    z2 = []
-    for i in range(TILES):
-        at = slice(i * 128, (i + 1) * 128)
-        spat_o[:, at] = (dot(w2t[...], r["taps2o"][:, at]) + bias).astype(BF)
-        here = pl.ds(i * 128, 128)
-        z2.append(send(spat_o.at[:, here], raw2.at[0, 1, zh, :, here], zp))
-    second(zh, r["taps2"])
-    raw2[0, 1, zh] = (dot(w2t[...], r["taps2"][...]) + bias).astype(BF)
-    own = raw2.at[0]
-    y2_own = to_frames(own, zh, 0, HALF2)
-    raw_k = [send(raw2.at[0, 1, zh], raw2.at[1, 1, zh], kp)]
-    wide = jnp.concatenate([raw2[0, 1, zh], spat_o[...]], axis=1).astype(F32)
-    q2_iota = lax.broadcasted_iota(jnp.int32, (Q2, 1), 0)
-    row3 = group_row(
-        jnp.sum(wide, axis=1, keepdims=True),
-        jnp.sum(wide * wide, axis=1, keepdims=True),
-        q2_iota + c * Q2,
-        C2 // GROUPS,
-    )
-    state = stat_send(row3, x_peers)
+            q2_iota + (2 * z + k) * Q2,
+            C2 // GROUPS,
+        )
+    state = stat_send(row3, xz_peers)
     par_k.wait_recv()
     cols3 = [cols, [to_columns(par[1, z]) for z in range(2)]]
-    y2_fwd = []
-
-    def share(tap, z, a, n):
-        here = pl.ds(a, n)
-        raw_k.append(send(raw2.at[0, tap, z, :, here], raw2.at[1, tap, z, :, here], kp))
-
-    def forward2(i):
-        z2[i].wait_recv()
-        y2_fwd.append(to_frames(own, oz, i * 128, 128))
-        share(1, oz, i * 128, 128)
-
     state = stat_send(stat_wait(state), y_peers)
-    for tap in (0, 2):
-        y2_own[tap // 2].wait_recv()
-        share(tap, zh, 0, HALF2)
-    forward2(0)
-    state = stat_send(stat_wait(state), chan_peers)
-    forward2(1)
-    forward2(2)
-    for i in range(TILES):
+    for z in range(2):
         for tap in (0, 2):
-            y2_fwd[i][tap // 2].wait_recv()
-            share(tap, oz, i * 128, 128)
+            y2[z][tap // 2].wait_recv()
+            raw_k.append(send(raw2.at[0, tap, z], raw2.at[1, tap, z], kp))
+    state = stat_send(stat_wait(state), [kp])
     total = stat_wait(state)
     hid2 = r["hid2"]
     for slot, core in ((0, k), (1, ok)):

time: 78.7 us -> 82.2 us (1.044)
  the two profiles are of different devices: /device:TPU:129 before, /device:TPU:67 now
where the time goes in v4:
time: 82.2 us; the launch traced here: 82.1 us
  Pallas kernels  80.4 us (98%)
  local copies, waits for them, and re-layouts  1.65 us (2%)
    pallas_call x1, Pallas kernels, per_device(): pl.pallas_call(functools.partial(kernel, frames), out_shape=jax.ShapeDtyp...  80.4 us
    unnamed x1, local copies, waits for them, and re-layouts  1.65 us

profile of v4, /device:TPU:67, one launch (start us, length us, event | category | flops | bytes accessed | tf_op | source)
XLA Modules:
  0.0 82.1 jit_solution(14709717836917420317)
XLA Ops:
  0.0 80.4 %video_block.1 = bf16[160,768]{1,0:T(8,128)(2,1)} custom-call(bf16[80,3072]{1,0:T(8,128)(2,1)} %bitcast.19, bf16[960,320]{1,0:T(8,128)(2,1)} %bitcast.17, f32[1,80]{1,0:T(1,128)} %bitcast.24, f32[1,80]{1,0:T(1,128)} %bitcast.25, bf16[720,320]{1,0:T(8,128)(2,1)} %bitcast.18, f32[320]{0:T(512)} %refs_5_.1, f32[320]{0:T(512)} %refs_6_.1, ...), custom_call_target="tpu_custom_call" | custom-call | tf_op jit(solution)/shard_map/video_block/pallas_call | solution.py:591
  80.4 1.7 %copy.15 = bf16[1,160,768]{2,1,0:T(8,128)(2,1)} copy(bf16[1,160,768]{2,1,0:T(8,128)(2,1)} %bitcast.16) | data formatting | bytes 491520

commit v5 on v3

--- a/solution.py
+++ b/solution.py
@@ -124,12 +124,19 @@
     kp = {"chan": c + 1 - 2 * k}
     after = {"frame": lax.rem(f + 1, frames)}
     before = {"frame": lax.rem(f + frames - 1, frames)}
-    chan_peers = [{"chan": lax.rem(c + d, 4)} for d in range(1, 4)]
     x_peers = [{"frame": lax.rem(x + d, NX) * ny + y} for d in range(1, NX)]
     y_peers = [{"frame": x * ny + lax.rem(y + d, ny)} for d in range(1, ny)]
 
+    xz_peers = [
+        {"frame": lax.rem(x + d, NX) * ny + y, "chan": lax.rem(c + e, 4)}
+        for d in range(NX)
+        for e in (0, 2)
+        if d or e
+    ]
+    y_pair = {"frame": x * ny + y + 1 - 2 * lax.rem(y, 2)}
+
     barrier = pltpu.get_barrier_semaphore()
-    greeted = chan_peers + x_peers + y_peers + [after, before]
+    greeted = xz_peers + y_peers + [kp, after, before]
     for peer in greeted:
         pl.semaphore_signal(barrier, inc=1, device_id=peer, device_id_type=MESH)
 
@@ -224,10 +231,10 @@
     dwt[zh, 9 * Q1 : DPAD, :] = jnp.zeros((DPAD - 9 * Q1, C1), BF)
     pl.semaphore_wait(barrier, len(greeted))
 
-    state = stat_send(row1, chan_peers)
-    pieces = ny // 2
-    piece = DPART // pieces
-    own_piece = pl.ds(pl.multiple_of(x * DPART + (y // 2) * piece, 16), piece)
+    state = stat_send(row1, xz_peers)
+    piece = DPART // 2
+    own_piece = pl.ds(pl.multiple_of(x * DPART + lax.rem(y, 2) * piece, 16), piece)
+    pair_piece = pl.ds(pl.multiple_of(x * DPART + lax.rem(y + 1, 2) * piece, 16), piece)
     dw_z = send(dwt.at[zh, own_piece], dwt.at[zh, own_piece], zp)
 
     z_copies = [
@@ -275,14 +282,6 @@
         r["pick1"][:, dx * 128 : (dx + 1) * 128] = jnp.where(
             same & (src_col == 2 * dst_col + dx - 1), 1.0, 0.0
         ).astype(BF)
-
-    state = stat_send(stat_wait(state), x_peers)
-    dw_z.wait_recv()
-    here = dwt.at[oz, own_piece]
-    dw_y = [
-        send(here, here, {"frame": x * ny + lax.rem(y + 2 * d, ny)}) for d in range(1, pieces)
-    ]
-    dw_x = [send(here, here, p) for p in x_peers]
 
     src = lax.broadcasted_iota(jnp.int32, (256, 256), 0)
     dst = lax.broadcasted_iota(jnp.int32, (256, 256), 1)
@@ -300,6 +299,11 @@
     for t in range(9):
         w2t[:, t * C1 : (t + 1) * C1] = r["cw2_v"][t * Q2 : (t + 1) * Q2, :]
     w2t[:, 9 * C1 : 10 * C1] = r["sw2_v"][...]
+    dw_z.wait_recv()
+    here = dwt.at[oz, own_piece]
+    dw_y = send(here, here, y_pair)
+    dw_x = [send(here, here, p) for p in x_peers]
+    state = stat_send(stat_wait(state), y_peers)
     y_fwd = []
 
     def forward(i):
@@ -307,18 +311,16 @@
         y_fwd.append(to_frames(raw1, oz, *CHUNKS[i]))
 
     forward(0)
-    state = stat_send(stat_wait(state), y_peers)
-    for d in range(1, pieces):
-        dw_y[d - 1].wait_recv()
-        start = x * DPART + lax.rem(y // 2 + pieces - d, pieces) * piece
-        there = dwt.at[oz, pl.ds(pl.multiple_of(start, 16), piece)]
-        dw_x += [send(there, there, p) for p in x_peers]
+    dw_y.wait_recv()
+    there = dwt.at[oz, pair_piece]
+    dw_x += [send(there, there, p) for p in x_peers]
     forward(1)
     loads["tw2"].wait()
     for slot, core in ((0, k), (1, ok)):
         prepare(r["tw2_v"], r["tmp2"], store4, C2, Q2, slot, core)
     par_copy.wait_recv()
     par_k = send(par.at[0], par.at[1], kp)
+    state = stat_send(stat_wait(state), [kp])
     cols = [to_columns(par[0, z]) for z in range(2)]
     cols2 = to_columns(r["par2"][...])
     bias = jnp.where(zh == 0, cols[0][0:Q2, 4:5], cols[1][0:Q2, 4:5])
@@ -422,20 +424,19 @@
         here = red.at[k, oz, :, pl.ds(i * 128, 128)]
         red_k[i].append(send(here, here, kp))
 
-    hid_own(0)
+    for i in range(3):
+        hid_own(i)
+    forward(2)
     hid_other(0)
-    hid_own(1)
-    forward(2)
+    hid_other(1)
     first_conv(0)
-    hid_other(1)
-    hid_own(2)
-    first_conv(1)
     for copy in dw_x:
         copy.wait_recv()
     down(0)
+    first_conv(1)
     down(1)
+    reduced(0)
     hid_other(2)
-    reduced(0)
     reduced(1)
     first_conv(2)
     down(2)
@@ -502,7 +503,7 @@
         q2_iota + c * Q2,
         C2 // GROUPS,
     )
-    state = stat_send(row3, x_peers)
+    state = stat_send(row3, xz_peers)
     par_k.wait_recv()
     cols3 = [cols, [to_columns(par[1, z]) for z in range(2)]]
     y2_fwd = []
@@ -516,14 +517,13 @@
         y2_fwd.append(to_frames(own, oz, i * 128, 128))
         share(1, oz, i * 128, 128)
 
-    state = stat_send(stat_wait(state), y_peers)
     for tap in (0, 2):
         y2_own[tap // 2].wait_recv()
         share(tap, zh, 0, HALF2)
-    forward2(0)
-    state = stat_send(stat_wait(state), chan_peers)
-    forward2(1)
-    forward2(2)
+    state = stat_send(stat_wait(state), y_peers)
+    for i in range(TILES):
+        forward2(i)
+    state = stat_send(stat_wait(state), [kp])
     for i in range(TILES):
         for tap in (0, 2):
             y2_fwd[i][tap // 2].wait_recv()

time: 78.7 us -> 82.7 us (1.051)
  Pallas kernels: 76.9 us -> 80.8 us
    pallas_call x1, Pallas kernels: 76.9 us -> 80.8 us  [per_device(): pl.pallas_call(functools.partial(kernel, frames), out_shape=jax.ShapeDtyp...]
where the time goes in v5:
time: 82.7 us; the launch traced here: 82.5 us
  Pallas kernels  80.8 us (98%)
  local copies, waits for them, and re-layouts  1.65 us (2%)
    pallas_call x1, Pallas kernels, per_device(): pl.pallas_call(functools.partial(kernel, frames), out_shape=jax.ShapeDtyp...  80.8 us

profile of v5, /device:TPU:129, one launch (start us, length us, event | category | flops | bytes accessed | tf_op | source)
XLA Modules:
  0.0 82.5 jit_solution(9990909689659090600)
XLA Ops:
  0.0 80.8 %video_block.1 = bf16[160,768]{1,0:T(8,128)(2,1)} custom-call(bf16[80,3072]{1,0:T(8,128)(2,1)} %bitcast.19, bf16[960,320]{1,0:T(8,128)(2,1)} %bitcast.17, f32[1,80]{1,0:T(1,128)} %bitcast.24, f32[1,80]{1,0:T(1,128)} %bitcast.25, bf16[720,320]{1,0:T(8,128)(2,1)} %bitcast.18, f32[320]{0:T(512)} %refs_5_.1, f32[320]{0:T(512)} %refs_6_.1, ...), custom_call_target="tpu_custom_call" | custom-call | tf_op jit(solution)/shard_map/video_block/pallas_call | solution.py:579
  80.8 1.7 %copy.15 = bf16[1,160,768]{2,1,0:T(8,128)(2,1)} copy(bf16[1,160,768]{2,1,0:T(8,128)(2,1)} %bitcast.16) | data formatting | bytes 491520

commit v6 on v3

--- a/solution.py
+++ b/solution.py
@@ -30,6 +30,7 @@
 DPART = DPAD // NX
 TILES = HALF2 // 128
 CHUNKS = ((0, 640), (640, 512), (1152, 512))
+CHUNKS2 = ((0, 384), (384, 256), (640, 128))
 
 SCRATCH = {
     "lat_v": ((Q1, H1 * W1), BF),
@@ -50,16 +51,14 @@
     "red": ((2, 2, C1 // 2, HALF2), BF),
     "nrm": ((C1, POS2 + 256), BF),
     "taps2": ((10 * C1, HALF2), BF),
-    "taps2o": ((10 * C1, HALF2), BF),
     "w2t": ((Q2, 10 * C1), BF),
-    "spat_o": ((Q2, HALF2), BF),
-    "raw2": ((2, 3, 2, Q2, HALF2), BF),
-    "hid2": ((2, 3, 2, Q2, HALF2), BF),
+    "raw2": ((2, 3, 2, Q2, POS2), BF),
+    "hid2": ((2, 3, 2, Q2, POS2), BF),
     "tmp2": ((C2, 6 * Q2), BF),
-    "w4t": ((2, 2, Q2, 6 * Q2), BF),
+    "w4t": ((2, Q2, 6 * Q2), BF),
     "pick1": ((256, 384), BF),
     "pick2": ((3, 256, 256), BF),
-    "fin": ((2, Q2, HALF2), BF),
+    "fin": ((Q2, POS2), BF),
     "par": ((2, 2, 8, 256), F32),
     "par2": ((8, 384), F32),
     "g1_v": ((1, Q1), F32),
@@ -128,8 +127,15 @@
     x_peers = [{"frame": lax.rem(x + d, NX) * ny + y} for d in range(1, NX)]
     y_peers = [{"frame": x * ny + lax.rem(y + d, ny)} for d in range(1, ny)]
 
+    xz_peers = [
+        {"frame": lax.rem(x + d, NX) * ny + y, "chan": lax.rem(c + e, 4)}
+        for d in range(NX)
+        for e in (0, 2)
+        if d or e
+    ]
+
     barrier = pltpu.get_barrier_semaphore()
-    greeted = chan_peers + x_peers + y_peers + [after, before]
+    greeted = chan_peers + xz_peers + y_peers + [after, before]
     for peer in greeted:
         pl.semaphore_signal(barrier, inc=1, device_id=peer, device_id_type=MESH)
 
@@ -225,9 +231,9 @@
     pl.semaphore_wait(barrier, len(greeted))
 
     state = stat_send(row1, chan_peers)
-    pieces = ny // 2
+    pieces = 2
     piece = DPART // pieces
-    own_piece = pl.ds(pl.multiple_of(x * DPART + (y // 2) * piece, 16), piece)
+    own_piece = pl.ds(pl.multiple_of(x * DPART + lax.rem(y, 2) * piece, 16), piece)
     dw_z = send(dwt.at[zh, own_piece], dwt.at[zh, own_piece], zp)
 
     z_copies = [
@@ -244,27 +250,23 @@
     y_own = [to_frames(raw1, zh, a, n) for a, n in CHUNKS]
     par_copy = send(par.at[0, zh], par.at[0, zh], zp)
 
-    def prepare(weight, held, store, width, count, slot, core):
+    def prepare(weight, held, width, count, core):
         rows = [
             weight[pl.ds(pl.multiple_of(t * width + z * 2 * count + core * count, 16), count), :]
             for t in range(3)
             for z in range(2)
         ]
         held[...] = jnp.concatenate(rows, axis=0).T
-        for z in range(2):
-            store(slot, z, held[pl.ds(pl.multiple_of(z * 2 * count + k * count, 16), count), :])
 
     w1t, w4t, w2t = r["w1t"], r["w4t"], r["w2t"]
-
-    def store1(slot, z, value):
-        w1t[slot, z * Q1 : (z + 1) * Q1, :] = value
-
-    def store4(slot, z, value):
-        w4t[slot, z] = value
 
     loads["tw1"].wait()
     for slot, core in ((0, k), (1, ok)):
-        prepare(r["tw1_v"], r["tmp1"], store1, C1, Q1, slot, core)
+        prepare(r["tw1_v"], r["tmp1"], C1, Q1, core)
+        for z in range(2):
+            w1t[slot, z * Q1 : (z + 1) * Q1, :] = r["tmp1"][
+                pl.ds(pl.multiple_of((2 * z + k) * Q1, 16), Q1), :
+            ]
 
     src = lax.broadcasted_iota(jnp.int32, (256, 128), 0)
     dst = lax.broadcasted_iota(jnp.int32, (256, 128), 1)
@@ -280,7 +282,7 @@
     dw_z.wait_recv()
     here = dwt.at[oz, own_piece]
     dw_y = [
-        send(here, here, {"frame": x * ny + lax.rem(y + 2 * d, ny)}) for d in range(1, pieces)
+        send(here, here, {"frame": x * ny + y + 1 - 2 * lax.rem(y, 2)}) for d in range(1, pieces)
     ]
     dw_x = [send(here, here, p) for p in x_peers]
 
@@ -310,13 +312,14 @@
     state = stat_send(stat_wait(state), y_peers)
     for d in range(1, pieces):
         dw_y[d - 1].wait_recv()
-        start = x * DPART + lax.rem(y // 2 + pieces - d, pieces) * piece
+        start = x * DPART + lax.rem(y + 1, 2) * piece
         there = dwt.at[oz, pl.ds(pl.multiple_of(start, 16), piece)]
         dw_x += [send(there, there, p) for p in x_peers]
     forward(1)
     loads["tw2"].wait()
     for slot, core in ((0, k), (1, ok)):
-        prepare(r["tw2_v"], r["tmp2"], store4, C2, Q2, slot, core)
+        prepare(r["tw2_v"], r["tmp2"], C2, Q2, core)
+        w4t[slot] = r["tmp2"][pl.ds(pl.multiple_of(c * Q2, 16), Q2), :]
     par_copy.wait_recv()
     par_k = send(par.at[0], par.at[1], kp)
     cols = [to_columns(par[0, z]) for z in range(2)]
@@ -469,7 +472,7 @@
     def second(side, taps):
         for dx in range(3):
             for j in range(TILES + 1):
-                window = nrm[:, lanes(side * HALF2 + j * 128, 256)]
+                window = nrm[:, side * HALF2 + j * 128 : side * HALF2 + j * 128 + 256]
                 got = dot(window, r["pick2"][dx]).astype(BF)
                 if j < TILES:
                     at = slice(j * 128, (j + 1) * 128)
@@ -481,20 +484,20 @@
         for core in range(2):
             taps[9 * C1 + core * half : 9 * C1 + (core + 1) * half, :] = red[core, side]
 
-    spat_o = r["spat_o"]
-    second(oz, r["taps2o"])
+    own = raw2.at[0]
     z2 = []
-    for i in range(TILES):
-        at = slice(i * 128, (i + 1) * 128)
-        spat_o[:, at] = (dot(w2t[...], r["taps2o"][:, at]) + bias).astype(BF)
-        here = pl.ds(i * 128, 128)
-        z2.append(send(spat_o.at[:, here], raw2.at[0, 1, zh, :, here], zp))
-    second(zh, r["taps2"])
-    raw2[0, 1, zh] = (dot(w2t[...], r["taps2"][...]) + bias).astype(BF)
-    own = raw2.at[0]
-    y2_own = to_frames(own, zh, 0, HALF2)
-    raw_k = [send(raw2.at[0, 1, zh], raw2.at[1, 1, zh], kp)]
-    wide = jnp.concatenate([raw2[0, 1, zh], spat_o[...]], axis=1).astype(F32)
+
+    def to_other(a, n):
+        here = own.at[1, zh, :, pl.ds(a, n)]
+        z2.append(send(here, here, zp))
+
+    for side in range(2):
+        second(side, r["taps2"])
+        at = slice(side * HALF2, (side + 1) * HALF2)
+        raw2[0, 1, zh, :, at] = (dot(w2t[...], r["taps2"][...]) + bias).astype(BF)
+        for a, n in CHUNKS2[:1] if side == 0 else CHUNKS2[1:]:
+            to_other(a, n)
+    wide = raw2[0, 1, zh].astype(F32)
     q2_iota = lax.broadcasted_iota(jnp.int32, (Q2, 1), 0)
     row3 = group_row(
         jnp.sum(wide, axis=1, keepdims=True),
@@ -502,40 +505,44 @@
         q2_iota + c * Q2,
         C2 // GROUPS,
     )
-    state = stat_send(row3, x_peers)
+    state = stat_send(row3, y_peers)
+    y2_own = to_frames(own, zh, 0, POS2)
+    raw_k = {a: [] for a, n in CHUNKS2}
+
+    def share(tap, z, a, n):
+        here = pl.ds(a, n)
+        raw_k[a].append(send(raw2.at[0, tap, z, :, here], raw2.at[1, tap, z, :, here], kp))
+
+    share(1, zh, 0, POS2)
     par_k.wait_recv()
     cols3 = [cols, [to_columns(par[1, z]) for z in range(2)]]
     y2_fwd = []
 
-    def share(tap, z, a, n):
-        here = pl.ds(a, n)
-        raw_k.append(send(raw2.at[0, tap, z, :, here], raw2.at[1, tap, z, :, here], kp))
-
     def forward2(i):
         z2[i].wait_recv()
-        y2_fwd.append(to_frames(own, oz, i * 128, 128))
-        share(1, oz, i * 128, 128)
-
-    state = stat_send(stat_wait(state), y_peers)
+        y2_fwd.append(to_frames(own, oz, *CHUNKS2[i]))
+        share(1, oz, *CHUNKS2[i])
+
+    def arrived(i):
+        for tap in (0, 2):
+            y2_fwd[i][tap // 2].wait_recv()
+            share(tap, oz, *CHUNKS2[i])
+
+    forward2(0)
+    state = stat_send(stat_wait(state), xz_peers)
+    forward2(1)
+    forward2(2)
     for tap in (0, 2):
         y2_own[tap // 2].wait_recv()
-        share(tap, zh, 0, HALF2)
-    forward2(0)
-    state = stat_send(stat_wait(state), chan_peers)
-    forward2(1)
-    forward2(2)
-    for i in range(TILES):
-        for tap in (0, 2):
-            y2_fwd[i][tap // 2].wait_recv()
-            share(tap, oz, i * 128, 128)
+        share(tap, zh, 0, POS2)
+    arrived(0)
+    state = stat_send(stat_wait(state), [kp])
+    arrived(1)
+    arrived(2)
     total = stat_wait(state)
-    hid2 = r["hid2"]
-    for slot, core in ((0, k), (1, ok)):
-        if slot == 1:
-            for copy in raw_k:
-                copy.wait_recv()
-        for z in range(2):
-            scale, shift = scale_columns(
+    affine3 = [
+        [
+            scale_columns(
                 total,
                 float(C2 // GROUPS * POS2 * frames),
                 q2_iota + (2 * z + core) * Q2,
@@ -543,32 +550,36 @@
                 cols3[slot][z][0:Q2, 2:3],
                 cols3[slot][z][0:Q2, 3:4],
             )
-            for tap in range(3):
-                value = silu_of_half(raw2[slot, tap, z].astype(F32) * scale + shift)
-                if tap != 1:
-                    value = jnp.where(alive[tap], value, 0.0)
-                hid2[slot, tap, z] = value.astype(BF)
-
-    fin = r["fin"]
-
-    def second_conv(z, at, n):
+            for z in range(2)
+        ]
+        for slot, core in ((0, k), (1, ok))
+    ]
+    hid2, fin = r["hid2"], r["fin"]
+    stores = []
+    for a, n in CHUNKS2:
+        at = slice(a, a + n)
+        for slot in range(2):
+            if slot == 1:
+                for copy in raw_k[a]:
+                    copy.wait_recv()
+            for z in range(2):
+                scale, shift = affine3[slot][z]
+                for tap in range(3):
+                    value = silu_of_half(raw2[slot, tap, z, :, at].astype(F32) * scale + shift)
+                    if tap != 1:
+                        value = jnp.where(alive[tap], value, 0.0)
+                    hid2[slot, tap, z, :, at] = value.astype(BF)
         mixed = sum(
-            dot(w4t[slot, z], hid2[slot, :, :, :, at].reshape(6 * Q2, n)) for slot in range(2)
+            dot(w4t[slot], hid2[slot, :, :, :, at].reshape(6 * Q2, n)) for slot in range(2)
         ).astype(BF)
-        return (raw2[0, 1, z, :, at].astype(F32) + mixed.astype(F32)).astype(BF)
-
-    last = []
-    for i in range(TILES):
-        at = slice(i * 128, (i + 1) * 128)
-        fin[0, :, at] = second_conv(oz, at, 128)
-        there = out.at[:, lanes(zh * HALF2 + i * 128, 128)]
-        last.append(send(fin.at[0, :, pl.ds(i * 128, 128)], there, zp))
-    fin[1] = second_conv(zh, slice(0, HALF2), HALF2)
-    kept = pltpu.make_async_copy(fin.at[1], out.at[:, lanes(zh * HALF2, HALF2)], local_sem.at[15])
-    kept.start()
-    for copy in last:
-        copy.wait_recv()
-    kept.wait()
+        fin[:, at] = (raw2[0, 1, zh, :, at].astype(F32) + mixed.astype(F32)).astype(BF)
+        here = pl.ds(a, n)
+        stores.append(
+            pltpu.make_async_copy(fin.at[:, here], out.at[:, here], local_sem.at[13 + len(stores)])
+        )
+        stores[-1].start()
+    for copy in stores:
+        copy.wait()
     for copy in sent:
         copy.wait_send()
 

time: 78.7 us -> 79.1 us (level)
  no operation moved by 1% of the time
where the time goes in v6:
time: 79.1 us; the launch traced here: 79 us
  Pallas kernels  77.3 us (98%)
  local copies, waits for them, and re-layouts  1.65 us (2%)
    pallas_call x1, Pallas kernels, per_device(): pl.pallas_call(functools.partial(kernel, frames), out_shape=jax.ShapeDtyp...  77.3 us
    unnamed x1, local copies, waits for them, and re-layouts  1.65 us

profile of v6, /device:TPU:129, one launch (start us, length us, event | category | flops | bytes accessed | tf_op | source)
XLA Modules:
  0.0 79.0 jit_solution(11925473201385173000)
XLA Ops:
  0.0 77.3 %video_block.1 = bf16[160,768]{1,0:T(8,128)(2,1)} custom-call(bf16[80,3072]{1,0:T(8,128)(2,1)} %bitcast.19, bf16[960,320]{1,0:T(8,128)(2,1)} %bitcast.17, f32[1,80]{1,0:T(1,128)} %bitcast.24, f32[1,80]{1,0:T(1,128)} %bitcast.25, bf16[720,320]{1,0:T(8,128)(2,1)} %bitcast.18, f32[320]{0:T(512)} %refs_5_.1, f32[320]{0:T(512)} %refs_6_.1, ...), custom_call_target="tpu_custom_call" | custom-call | tf_op jit(solution)/shard_map/video_block/pallas_call | solution.py:590
  77.3 1.7 %copy.15 = bf16[1,160,768]{2,1,0:T(8,128)(2,1)} copy(bf16[1,160,768]{2,1,0:T(8,128)(2,1)} %bitcast.16) | data formatting | bytes 491520

commit v7 on v6

--- a/solution.py
+++ b/solution.py
@@ -278,7 +278,6 @@
             same & (src_col == 2 * dst_col + dx - 1), 1.0, 0.0
         ).astype(BF)
 
-    state = stat_send(stat_wait(state), x_peers)
     dw_z.wait_recv()
     here = dwt.at[oz, own_piece]
     dw_y = [
@@ -286,6 +285,7 @@
     ]
     dw_x = [send(here, here, p) for p in x_peers]
 
+    state = stat_send(stat_wait(state), x_peers)
     src = lax.broadcasted_iota(jnp.int32, (256, 256), 0)
     dst = lax.broadcasted_iota(jnp.int32, (256, 256), 1)
     second = dst >= 128
@@ -308,13 +308,13 @@
         z_copies[i].wait_recv()
         y_fwd.append(to_frames(raw1, oz, *CHUNKS[i]))
 
-    forward(0)
-    state = stat_send(stat_wait(state), y_peers)
     for d in range(1, pieces):
         dw_y[d - 1].wait_recv()
         start = x * DPART + lax.rem(y + 1, 2) * piece
         there = dwt.at[oz, pl.ds(pl.multiple_of(start, 16), piece)]
         dw_x += [send(there, there, p) for p in x_peers]
+    forward(0)
+    state = stat_send(stat_wait(state), y_peers)
     forward(1)
     loads["tw2"].wait()
     for slot, core in ((0, k), (1, ok)):

time: 79.1 us -> 82.6 us (1.044)
  the two profiles are of different devices: /device:TPU:129 before, /device:TPU:131 now
where the time goes in v7:
time: 82.6 us; the launch traced here: 82.4 us
  Pallas kernels  80.8 us (98%)
  local copies, waits for them, and re-layouts  1.65 us (2%)
    pallas_call x1, Pallas kernels, per_device(): pl.pallas_call(functools.partial(kernel, frames), out_shape=jax.ShapeDtyp...  80.8 us
    unnamed x1, local copies, waits for them, and re-layouts  1.65 us

profile of v7, /device:TPU:131, one launch (start us, length us, event | category | flops | bytes accessed | tf_op | source)
XLA Modules:
  0.0 82.4 jit_solution(17799600660737274934)
XLA Ops:
  0.0 80.8 %video_block.1 = bf16[160,768]{1,0:T(8,128)(2,1)} custom-call(bf16[80,3072]{1,0:T(8,128)(2,1)} %bitcast.19, bf16[960,320]{1,0:T(8,128)(2,1)} %bitcast.17, f32[1,80]{1,0:T(1,128)} %bitcast.24, f32[1,80]{1,0:T(1,128)} %bitcast.25, bf16[720,320]{1,0:T(8,128)(2,1)} %bitcast.18, f32[320]{0:T(512)} %refs_5_.1, f32[320]{0:T(512)} %refs_6_.1, ...), custom_call_target="tpu_custom_call" | custom-call | tf_op jit(solution)/shard_map/video_block/pallas_call | solution.py:590
  80.8 1.7 %copy.15 = bf16[1,160,768]{2,1,0:T(8,128)(2,1)} copy(bf16[1,160,768]{2,1,0:T(8,128)(2,1)} %bitcast.16) | data formatting | bytes 491520

commit v8 on v6

--- a/solution.py
+++ b/solution.py
@@ -127,15 +127,8 @@
     x_peers = [{"frame": lax.rem(x + d, NX) * ny + y} for d in range(1, NX)]
     y_peers = [{"frame": x * ny + lax.rem(y + d, ny)} for d in range(1, ny)]
 
-    xz_peers = [
-        {"frame": lax.rem(x + d, NX) * ny + y, "chan": lax.rem(c + e, 4)}
-        for d in range(NX)
-        for e in (0, 2)
-        if d or e
-    ]
-
     barrier = pltpu.get_barrier_semaphore()
-    greeted = chan_peers + xz_peers + y_peers + [after, before]
+    greeted = chan_peers + x_peers + y_peers + [after, before]
     for peer in greeted:
         pl.semaphore_signal(barrier, inc=1, device_id=peer, device_id_type=MESH)
 
@@ -231,9 +224,9 @@
     pl.semaphore_wait(barrier, len(greeted))
 
     state = stat_send(row1, chan_peers)
-    pieces = 2
+    pieces = ny // 2
     piece = DPART // pieces
-    own_piece = pl.ds(pl.multiple_of(x * DPART + lax.rem(y, 2) * piece, 16), piece)
+    own_piece = pl.ds(pl.multiple_of(x * DPART + (y // 2) * piece, 16), piece)
     dw_z = send(dwt.at[zh, own_piece], dwt.at[zh, own_piece], zp)
 
     z_copies = [
@@ -282,7 +275,7 @@
     dw_z.wait_recv()
     here = dwt.at[oz, own_piece]
     dw_y = [
-        send(here, here, {"frame": x * ny + y + 1 - 2 * lax.rem(y, 2)}) for d in range(1, pieces)
+        send(here, here, {"frame": x * ny + lax.rem(y + 2 * d, ny)}) for d in range(1, pieces)
     ]
     dw_x = [send(here, here, p) for p in x_peers]
 
@@ -312,7 +305,7 @@
     state = stat_send(stat_wait(state), y_peers)
     for d in range(1, pieces):
         dw_y[d - 1].wait_recv()
-        start = x * DPART + lax.rem(y + 1, 2) * piece
+        start = x * DPART + lax.rem(y // 2 + pieces - d, pieces) * piece
         there = dwt.at[oz, pl.ds(pl.multiple_of(start, 16), piece)]
         dw_x += [send(there, there, p) for p in x_peers]
     forward(1)
@@ -497,6 +490,7 @@
         raw2[0, 1, zh, :, at] = (dot(w2t[...], r["taps2"][...]) + bias).astype(BF)
         for a, n in CHUNKS2[:1] if side == 0 else CHUNKS2[1:]:
             to_other(a, n)
+    y2_own = to_frames(own, zh, 0, POS2)
     wide = raw2[0, 1, zh].astype(F32)
     q2_iota = lax.broadcasted_iota(jnp.int32, (Q2, 1), 0)
     row3 = group_row(
@@ -505,8 +499,7 @@
         q2_iota + c * Q2,
         C2 // GROUPS,
     )
-    state = stat_send(row3, y_peers)
-    y2_own = to_frames(own, zh, 0, POS2)
+    state = stat_send(row3, x_peers)
     raw_k = {a: [] for a, n in CHUNKS2}
 
     def share(tap, z, a, n):
@@ -528,17 +521,16 @@
             y2_fwd[i][tap // 2].wait_recv()
             share(tap, oz, *CHUNKS2[i])
 
+    state = stat_send(stat_wait(state), y_peers)
     forward2(0)
-    state = stat_send(stat_wait(state), xz_peers)
-    forward2(1)
-    forward2(2)
     for tap in (0, 2):
         y2_own[tap // 2].wait_recv()
         share(tap, zh, 0, POS2)
-    arrived(0)
-    state = stat_send(stat_wait(state), [kp])
-    arrived(1)
-    arrived(2)
+    state = stat_send(stat_wait(state), chan_peers)
+    forward2(1)
+    forward2(2)
+    for i in range(3):
+        arrived(i)
     total = stat_wait(state)
     affine3 = [
         [

time: 79.1 us -> 77.2 us (0.976)
  Pallas kernels: 77.3 us -> 75.4 us
    pallas_call x1, Pallas kernels: 77.3 us -> 75.4 us  [per_device(): pl.pallas_call(functools.partial(kernel, frames), out_shape=jax.ShapeDtyp...]
where the time goes in v8:
time: 77.2 us; the launch traced here: 77.1 us
  Pallas kernels  75.4 us (98%)
  local copies, waits for them, and re-layouts  1.65 us (2%)
    pallas_call x1, Pallas kernels, per_device(): pl.pallas_call(functools.partial(kernel, frames), out_shape=jax.ShapeDtyp...  75.4 us
    unnamed x1, local copies, waits for them, and re-layouts  1.65 us

profile of v8, /device:TPU:129, one launch (start us, length us, event | category | flops | bytes accessed | tf_op | source)
XLA Modules:
  0.0 77.1 jit_solution(734778358852226327)
XLA Ops:
  0.0 75.4 %video_block.1 = bf16[160,768]{1,0:T(8,128)(2,1)} custom-call(bf16[80,3072]{1,0:T(8,128)(2,1)} %bitcast.19, bf16[960,320]{1,0:T(8,128)(2,1)} %bitcast.17, f32[1,80]{1,0:T(1,128)} %bitcast.24, f32[1,80]{1,0:T(1,128)} %bitcast.25, bf16[720,320]{1,0:T(8,128)(2,1)} %bitcast.18, f32[320]{0:T(512)} %refs_5_.1, f32[320]{0:T(512)} %refs_6_.1, ...), custom_call_target="tpu_custom_call" | custom-call | tf_op jit(solution)/shard_map/video_block/pallas_call | solution.py:582
  75.5 1.7 %copy.15 = bf16[1,160,768]{2,1,0:T(8,128)(2,1)} copy(bf16[1,160,768]{2,1,0:T(8,128)(2,1)} %bitcast.16) | data formatting | bytes 491520

commit v9 on v8

--- a/solution.py
+++ b/solution.py
@@ -484,13 +484,21 @@
         here = own.at[1, zh, :, pl.ds(a, n)]
         z2.append(send(here, here, zp))
 
+    raw_k = {a: [] for a, n in CHUNKS2}
+    y2_own = []
+
+    def share(tap, z, a, n):
+        here = pl.ds(a, n)
+        raw_k[a].append(send(raw2.at[0, tap, z, :, here], raw2.at[1, tap, z, :, here], kp))
+
     for side in range(2):
         second(side, r["taps2"])
         at = slice(side * HALF2, (side + 1) * HALF2)
         raw2[0, 1, zh, :, at] = (dot(w2t[...], r["taps2"][...]) + bias).astype(BF)
         for a, n in CHUNKS2[:1] if side == 0 else CHUNKS2[1:]:
             to_other(a, n)
-    y2_own = to_frames(own, zh, 0, POS2)
+        y2_own.append(to_frames(own, zh, side * HALF2, HALF2))
+        share(1, zh, side * HALF2, HALF2)
     wide = raw2[0, 1, zh].astype(F32)
     q2_iota = lax.broadcasted_iota(jnp.int32, (Q2, 1), 0)
     row3 = group_row(
@@ -500,13 +508,6 @@
         C2 // GROUPS,
     )
     state = stat_send(row3, x_peers)
-    raw_k = {a: [] for a, n in CHUNKS2}
-
-    def share(tap, z, a, n):
-        here = pl.ds(a, n)
-        raw_k[a].append(send(raw2.at[0, tap, z, :, here], raw2.at[1, tap, z, :, here], kp))
-
-    share(1, zh, 0, POS2)
     par_k.wait_recv()
     cols3 = [cols, [to_columns(par[1, z]) for z in range(2)]]
     y2_fwd = []
@@ -523,9 +524,10 @@
 
     state = stat_send(stat_wait(state), y_peers)
     forward2(0)
-    for tap in (0, 2):
-        y2_own[tap // 2].wait_recv()
-        share(tap, zh, 0, POS2)
+    for side in range(2):
+        for tap in (0, 2):
+            y2_own[side][tap // 2].wait_recv()
+            share(tap, zh, side * HALF2, HALF2)
     state = stat_send(stat_wait(state), chan_peers)
     forward2(1)
     forward2(2)

time: 77.2 us -> 76.2 us (0.987)
  the two profiles are of different devices: /device:TPU:129 before, /device:TPU:66 now
where the time goes in v9:
time: 76.2 us; the launch traced here: 76 us
  Pallas kernels  74.4 us (98%)
  local copies, waits for them, and re-layouts  1.65 us (2%)
    pallas_call x1, Pallas kernels, per_device(): pl.pallas_call(functools.partial(kernel, frames), out_shape=jax.ShapeDtyp...  74.4 us
    unnamed x1, local copies, waits for them, and re-layouts  1.65 us

profile of v9, /device:TPU:66, one launch (start us, length us, event | category | flops | bytes accessed | tf_op | source)
XLA Modules:
  0.0 76.0 jit_solution(13042311573521929159)
XLA Ops:
  0.0 74.4 %video_block.1 = bf16[160,768]{1,0:T(8,128)(2,1)} custom-call(bf16[80,3072]{1,0:T(8,128)(2,1)} %bitcast.19, bf16[960,320]{1,0:T(8,128)(2,1)} %bitcast.17, f32[1,80]{1,0:T(1,128)} %bitcast.24, f32[1,80]{1,0:T(1,128)} %bitcast.25, bf16[720,320]{1,0:T(8,128)(2,1)} %bitcast.18, f32[320]{0:T(512)} %refs_5_.1, f32[320]{0:T(512)} %refs_6_.1, ...), custom_call_target="tpu_custom_call" | custom-call | tf_op jit(solution)/shard_map/video_block/pallas_call | solution.py:584
  74.4 1.7 %copy.15 = bf16[1,160,768]{2,1,0:T(8,128)(2,1)} copy(bf16[1,160,768]{2,1,0:T(8,128)(2,1)} %bitcast.16) | data formatting | bytes 491520
